TPU v7x, 32 devices: a whole 2x2x4 slice. The times are simulated.
32 devices in a mesh: clip: 8 (over z, x), sp: 4 (over y, core).
Axes of the slice: x: 2, y: 2, z: 4, core: 2. Of those that a mesh axis runs over, the one named last changes fastest.
Arguments:
- features: bfloat16 [32, 4, 28, 28, 1024], P('clip', None, 'sp'), may hold values from -12 to 12
- strides: int32 [32], replicated, may hold values from 1 to 4, as said below
- cotangent: bfloat16 [32, 4, 28, 28, 1024], P('clip', None, 'sp'), may hold values from -6 to 6
- w_reduce: bfloat16 [2, 1024, 256], P(None, ('clip', 'sp')), may hold values from -0.1875 to 0.1875
- w_mix: bfloat16 [2, 256, 256], P(None, ('clip', 'sp')), may hold values from -0.375 to 0.375
- w_expand: bfloat16 [2, 256, 1024], P(None, ('clip', 'sp')), may hold values from -0.375 to 0.375
- w_depth: bfloat16 [2, 27, 256], P(None, None, ('clip', 'sp')), may hold values from -1.25 to 1.25
- gains_mid: bfloat16 [2, 2, 256], P(None, None, ('clip', 'sp')), may hold values from 0.25 to 1.75
- biases_mid: bfloat16 [2, 2, 256], P(None, None, ('clip', 'sp')), may hold values from -2 to 2
- gains_out: bfloat16 [2, 1024], P(None, ('clip', 'sp')), may hold values from 0.25 to 1.75
- biases_out: bfloat16 [2, 1024], P(None, ('clip', 'sp')), may hold values from -2 to 2
Outputs:
- output: bfloat16 [32, 4, 28, 28, 1024], P('clip', None, 'sp')
- input_grad: bfloat16 [32, 4, 28, 28, 1024], P('clip', None, 'sp')
- grad_reduce: float32 [2, 1024, 256], P(None, ('clip', 'sp'))
- grad_mix: float32 [2, 256, 256], P(None, ('clip', 'sp'))
- grad_expand: float32 [2, 256, 1024], P(None, ('clip', 'sp'))
- grad_depth: float32 [2, 27, 256], P(None, None, ('clip', 'sp'))
- grad_gains_mid: float32 [2, 2, 256], P(None, None, ('clip', 'sp'))
- grad_biases_mid: float32 [2, 2, 256], P(None, None, ('clip', 'sp'))
- grad_gains_out: float32 [2, 1024], P(None, ('clip', 'sp'))
- grad_biases_out: float32 [2, 1024], P(None, ('clip', 'sp'))
Inputs may be any that keep to these rules, and one draw needn't show every extreme that they name: `strides`: each clip's stride is 1, 2 or 4, and it has 4 // stride valid frames; some clip has stride 1 and some stride 4.
All inputs are finite; a program needn't handle non-finite values.
Results may differ from a plain program's by a relative error of at most 0.02.
Values may be sent and summed in bfloat16 or wider, within the bound.
No kernel may reach another device: no remote copies, remote signals or barrier semaphores. Data moves between devices by JAX's collectives and lax.ppermute only.
A program may use at most 256 MiB of HBM per device.

v0:
```python
import jax
import jax.numpy as jnp
from jax import lax
from jax.sharding import PartitionSpec as P

epsilon = 1e-05


def padded_2(value, sides, width):
    for axis, dim in sides:
        peers, length = (lax.axis_size(axis), value.shape[dim])
        up = [(i, (i + 1) % peers) for i in range(peers - 1)]
        down = [(j, i) for i, j in up]
        last = lax.slice_in_dim(value, length - width, length, axis=dim)
        leading = lax.slice_in_dim(value, 0, width, axis=dim)
        before = lax.ppermute(last, axis, up)
        after = lax.ppermute(leading, axis, down)
        value = jnp.concatenate([before, value, after], axis=dim)
    return value


def silu_slope(source):
    sigma = jax.nn.sigmoid(source)
    return sigma * (1.0 + source * (1.0 - sigma))


def channel_sum(source):
    return jnp.sum(source, axis=(0, 1, 2, 3))


def moments(source, valid_mask, voxel_count):
    amount = lax.psum(channel_sum(source * valid_mask), ("clip", "sp"))
    mean_value = amount / voxel_count
    center = source - mean_value
    spread = lax.psum(channel_sum(center * center * valid_mask), ("clip", "sp")) / voxel_count
    return (mean_value, lax.rsqrt(spread + epsilon))


def norm_back(upstream, normed, gain_value, inverse_std, valid_mask, voxel_count):
    sum_out, sum_along = lax.psum(
        (channel_sum(upstream), channel_sum(upstream * normed)), ("clip", "sp")
    )
    inner = (upstream - sum_out / voxel_count - normed * (sum_along / voxel_count)) * valid_mask
    return (inverse_std * gain_value * inner, sum_out, sum_along)


def frame_pad(field):
    return jnp.pad(field, ((0, 0), (1, 1), (0, 0), (1, 1), (0, 0)))


def depth_forward(padded, kernel, frames, row_count, columns):
    result = None
    for offset in range(27):
        frame_step, row_step, column_step = (offset // 9, offset // 3 % 3, offset % 3)
        term = (
            kernel[offset]
            * padded[
                :,
                frame_step : frame_step + frames,
                row_step : row_step + row_count,
                column_step : column_step + columns,
            ]
        )
        result = term if result is None else result + term
    return result


def depth_back(grad_padded, kept_padded, kernel, frames, row_count, columns):
    own_grad = grad_padded[:, 1 : 1 + frames, 1 : 1 + row_count, 1 : 1 + columns].astype(
        jnp.float32
    )
    result = None
    kernel_terms = []
    for offset in range(27):
        frame_step, row_step, column_step = (offset // 9, offset // 3 % 3, offset % 3)
        shifted = grad_padded[
            :,
            2 - frame_step : 2 - frame_step + frames,
            2 - row_step : 2 - row_step + row_count,
            2 - column_step : 2 - column_step + columns,
        ]
        term = kernel[offset] * shifted
        result = term if result is None else result + term
        kernel_terms.append(
            channel_sum(
                own_grad
                * kept_padded[
                    :,
                    frame_step : frame_step + frames,
                    row_step : row_step + row_count,
                    column_step : column_step + columns,
                ]
            )
        )
    return (result, jnp.stack(kernel_terms))


def flat_product(left_side, right_side):
    left_flat = left_side.reshape(-1, left_side.shape[-1])
    right_flat = right_side.reshape(-1, right_side.shape[-1])
    return lax.dot_general(
        left_flat, right_flat, (((0,), (0,)), ((), ())), preferred_element_type=jnp.float32
    )


def back_product(grad_field, weight):
    return lax.dot_general(
        grad_field, weight, (((4,), (1,)), ((), ())), preferred_element_type=jnp.float32
    )


def fetch_forward(params, layer):
    return (
        lax.all_gather(params[0][layer], ("clip", "sp"), axis=0, tiled=True),
        lax.all_gather(params[1][layer], ("clip", "sp"), axis=0, tiled=True),
        lax.all_gather(params[2][layer], ("clip", "sp"), axis=0, tiled=True),
        lax.all_gather(params[3][layer], ("clip", "sp"), axis=1, tiled=True),
        lax.all_gather(params[4][layer], ("clip", "sp"), axis=1, tiled=True),
        lax.all_gather(params[5][layer], ("clip", "sp"), axis=1, tiled=True),
        lax.all_gather(params[6][layer], ("clip", "sp"), axis=0, tiled=True),
        lax.all_gather(params[7][layer], ("clip", "sp"), axis=0, tiled=True),
    )


def fetch_again(params, layer):
    return (
        lax.all_gather(params[0][layer], ("clip", "sp"), axis=0, tiled=True),
        lax.all_gather(params[1][layer], ("clip", "sp"), axis=0, tiled=True),
        lax.all_gather(params[2][layer], ("clip", "sp"), axis=0, tiled=True),
        lax.all_gather(params[3][layer], ("clip", "sp"), axis=1, tiled=True),
        lax.all_gather(params[4][layer], ("clip", "sp"), axis=1, tiled=True),
        lax.all_gather(params[5][layer], ("clip", "sp"), axis=1, tiled=True),
        lax.all_gather(params[6][layer], ("clip", "sp"), axis=0, tiled=True),
        lax.all_gather(params[7][layer], ("clip", "sp"), axis=0, tiled=True),
    )


def forward_block(low_input, residual, weights, valid_mask, voxel_count):
    w_first, w_second, w_third, kernel, gain_mid, bias_mid, gain_out, bias_out = weights
    kernel = kernel.astype(jnp.float32)
    gain_mid = gain_mid.astype(jnp.float32)
    bias_mid = bias_mid.astype(jnp.float32)
    gain_out = gain_out.astype(jnp.float32)
    bias_out = bias_out.astype(jnp.float32)
    reduced = jnp.dot(low_input, w_first, preferred_element_type=jnp.float32)
    mean_first, inverse_first = moments(reduced, valid_mask, voxel_count)
    normed_first = (reduced - mean_first) * inverse_first
    hidden_first = (valid_mask * jax.nn.silu(gain_mid[0] * normed_first + bias_mid[0])).astype(
        jnp.bfloat16
    )
    mixed_field = jnp.dot(hidden_first, w_second, preferred_element_type=jnp.float32).astype(
        jnp.bfloat16
    )
    framed = frame_pad(padded_2(mixed_field, (("sp", 2),), 1))
    frames, row_count, columns = (mixed_field.shape[1], mixed_field.shape[2], mixed_field.shape[3])
    spatial = depth_forward(framed, kernel, frames, row_count, columns)
    mean_second, inverse_second = moments(spatial, valid_mask, voxel_count)
    normed_second = (spatial - mean_second) * inverse_second
    hidden_second = (valid_mask * jax.nn.silu(gain_mid[1] * normed_second + bias_mid[1])).astype(
        jnp.bfloat16
    )
    expanded = jnp.dot(hidden_second, w_third, preferred_element_type=jnp.float32)
    mean_third, inverse_third = moments(expanded, valid_mask, voxel_count)
    normed_third = (expanded - mean_third) * inverse_third
    summed = residual + gain_out * normed_third + bias_out
    result = valid_mask * jax.nn.silu(summed)
    stored = (
        low_input,
        normed_first,
        inverse_first,
        hidden_first,
        framed,
        normed_second,
        inverse_second,
        hidden_second,
        normed_third,
        inverse_third,
        summed,
    )
    return (stored, result)


def backward_block(upstream, stored, weights, valid_mask, voxel_count):
    (
        low_input,
        normed_first,
        inverse_first,
        hidden_first,
        framed,
        normed_second,
        inverse_second,
        hidden_second,
        normed_third,
        inverse_third,
        summed,
    ) = stored
    w_first, w_second, w_third, kernel, gain_mid, bias_mid, gain_out, bias_out = weights
    kernel = kernel.astype(jnp.float32)
    gain_mid = gain_mid.astype(jnp.float32)
    bias_mid = bias_mid.astype(jnp.float32)
    gain_out = gain_out.astype(jnp.float32)
    grad_summed = upstream * valid_mask * silu_slope(summed)
    grad_expanded, sum_third, along_third = norm_back(
        grad_summed, normed_third, gain_out, inverse_third, valid_mask, voxel_count
    )
    grad_expanded = grad_expanded.astype(jnp.bfloat16)
    grad_third = flat_product(hidden_second, grad_expanded)
    grad_hidden_second = back_product(grad_expanded, w_third)
    grad_inner_second = (
        grad_hidden_second * valid_mask * silu_slope(gain_mid[1] * normed_second + bias_mid[1])
    )
    grad_spatial, sum_second, along_second = norm_back(
        grad_inner_second, normed_second, gain_mid[1], inverse_second, valid_mask, voxel_count
    )
    grad_spatial = grad_spatial.astype(jnp.bfloat16)
    grad_framed = frame_pad(padded_2(grad_spatial, (("sp", 2),), 1))
    frames, row_count, columns = (
        grad_spatial.shape[1],
        grad_spatial.shape[2],
        grad_spatial.shape[3],
    )
    grad_mixed, grad_kernel = depth_back(grad_framed, framed, kernel, frames, row_count, columns)
    grad_mixed = grad_mixed.astype(jnp.bfloat16)
    grad_second = flat_product(hidden_first, grad_mixed)
    grad_hidden_first = back_product(grad_mixed, w_second)
    grad_inner_first = (
        grad_hidden_first * valid_mask * silu_slope(gain_mid[0] * normed_first + bias_mid[0])
    )
    grad_reduced, sum_first, along_first = norm_back(
        grad_inner_first, normed_first, gain_mid[0], inverse_first, valid_mask, voxel_count
    )
    grad_reduced = grad_reduced.astype(jnp.bfloat16)
    grad_first = flat_product(low_input, grad_reduced)
    grad_input = grad_summed + back_product(grad_reduced, w_first)
    shards = (
        lax.psum_scatter(grad_first, ("clip", "sp"), scatter_dimension=0, tiled=True),
        lax.psum_scatter(grad_second, ("clip", "sp"), scatter_dimension=0, tiled=True),
        lax.psum_scatter(grad_third, ("clip", "sp"), scatter_dimension=0, tiled=True),
        lax.psum_scatter(grad_kernel, ("clip", "sp"), scatter_dimension=1, tiled=True),
    )
    norm_sums = (
        jnp.stack((along_first, along_second)),
        jnp.stack((sum_first, sum_second)),
        along_third,
        sum_third,
    )
    return (grad_input, shards, norm_sums)


def on_device(
    features,
    strides,
    cotangent,
    w_reduce,
    w_mix,
    w_expand,
    w_depth,
    gains_mid,
    biases_mid,
    gains_out,
    biases_out,
):
    params = (w_reduce, w_mix, w_expand, w_depth, gains_mid, biases_mid, gains_out, biases_out)
    clips_here, frames, row_count, columns = (
        features.shape[0],
        features.shape[1],
        features.shape[2],
        features.shape[3],
    )
    frame_counts = frames // strides
    voxel_count = (jnp.sum(frame_counts) * (row_count * lax.axis_size("sp") * columns)).astype(
        jnp.float32
    )
    local_frames = lax.dynamic_slice_in_dim(
        frame_counts, lax.axis_index("clip") * clips_here, clips_here
    )
    valid_mask = (
        lax.broadcasted_iota(jnp.int32, (clips_here, frames), 1) < local_frames[:, None]
    ).astype(jnp.float32)[:, :, None, None, None]
    position = lax.axis_index("clip") * lax.axis_size("sp") + lax.axis_index("sp")
    stored_all = []
    gathered = []
    current = features.astype(jnp.float32)
    low_input = features
    for layer in range(2):
        weights = fetch_forward(params, layer)
        gathered.append(weights)
        stored, current = forward_block(low_input, current, weights, valid_mask, voxel_count)
        stored_all.append(stored)
        low_input = current.astype(jnp.bfloat16)
    output = current.astype(jnp.bfloat16)
    upstream = cotangent.astype(jnp.float32)
    results = [None, None]
    for layer in (1, 0):
        weights = fetch_again(params, layer)
        upstream, shards, norm_sums = backward_block(
            upstream, stored_all[layer], weights, valid_mask, voxel_count
        )
        results[layer] = (shards, norm_sums)
    mid_width = gains_mid.shape[2]
    out_width = gains_out.shape[1]
    grad_reduce = jnp.stack((results[0][0][0], results[1][0][0]))
    grad_mix = jnp.stack((results[0][0][1], results[1][0][1]))
    grad_expand = jnp.stack((results[0][0][2], results[1][0][2]))
    grad_depth = jnp.stack((results[0][0][3], results[1][0][3]))
    grad_gains_mid = jnp.stack(
        tuple(
            (
                lax.dynamic_slice_in_dim(
                    results[layer][1][0], position * mid_width, mid_width, axis=1
                )
                for layer in range(2)
            )
        )
    )
    grad_biases_mid = jnp.stack(
        tuple(
            (
                lax.dynamic_slice_in_dim(
                    results[layer][1][1], position * mid_width, mid_width, axis=1
                )
                for layer in range(2)
            )
        )
    )
    grad_gains_out = jnp.stack(
        tuple(
            (
                lax.dynamic_slice_in_dim(results[layer][1][2], position * out_width, out_width)
                for layer in range(2)
            )
        )
    )
    grad_biases_out = jnp.stack(
        tuple(
            (
                lax.dynamic_slice_in_dim(results[layer][1][3], position * out_width, out_width)
                for layer in range(2)
            )
        )
    )
    return (
        output,
        upstream.astype(jnp.bfloat16),
        grad_reduce,
        grad_mix,
        grad_expand,
        grad_depth,
        grad_gains_mid,
        grad_biases_mid,
        grad_gains_out,
        grad_biases_out,
    )


def solution(mesh):
    return jax.shard_map(
        on_device,
        mesh=mesh,
        in_specs=(
            P("clip", None, "sp", None, None),
            P(),
            P("clip", None, "sp", None, None),
            P(None, ("clip", "sp"), None),
            P(None, ("clip", "sp"), None),
            P(None, ("clip", "sp"), None),
            P(None, None, ("clip", "sp")),
            P(None, None, ("clip", "sp")),
            P(None, None, ("clip", "sp")),
            P(None, ("clip", "sp")),
            P(None, ("clip", "sp")),
        ),
        out_specs=(
            P("clip", None, "sp", None, None),
            P("clip", None, "sp", None, None),
            P(None, ("clip", "sp"), None),
            P(None, ("clip", "sp"), None),
            P(None, ("clip", "sp"), None),
            P(None, None, ("clip", "sp")),
            P(None, None, ("clip", "sp")),
            P(None, None, ("clip", "sp")),
            P(None, ("clip", "sp")),
            P(None, ("clip", "sp")),
        ),
        check_vma=False,
    )
```

profile of v0, /device:TPU:0, one launch (start us, length us, event | category | flops | bytes accessed | tf_op | source)
XLA Modules:
  0.0 2336.3 jit_solution(13516443066079267355)
XLA Ops:
  12.4 43.5 %all-gather.1 = bf16[1,2,256]{1,0,2:T(2,128)(2,1)S(1)} all-gather(bf16[1,2,8]{1,0,2:T(2,128)(2,1)S(1)} %copy.89), channel_id=3, replica_groups=mesh['clip'=8,'sp'=4] {'clip','sp'}, dimensions={2}, use_global_device_ids=true | all-gather | bytes 1056 | tf_op jit(solution)/shard_map/all_gather | solution.py:118
  226.4 42.7 %psum.169 = f32[256]{0:T(256)S(1)} all-reduce(f32[256]{0:T(256)S(1)} %multiply_reduce_fusion.16), channel_id=1, replica_groups=mesh['clip'=8,'sp'=4] {'clip','sp'}, use_global_device_ids=true, to_apply=%region_4.5 | all-reduce | flops 256 | bytes 2048 | tf_op jit(solution)/shard_map/psum | solution.py:35
  277.2 42.5 %all-gather.10 = bf16[1,27,256]{1,2,0:T(8,128)(2,1)S(1)} all-gather(bf16[1,27,8]{1,2,0:T(8,128)(2,1)S(1)} %get-tuple-element.238), channel_id=12, replica_groups=mesh['clip'=8,'sp'=4] {'clip','sp'}, dimensions={2}, use_global_device_ids=true | all-gather | bytes 14256 | tf_op jit(solution)/shard_map/all_gather | solution.py:117
  403.5 41.7 %all-gather.13 = bf16[1,256,256]{2,1,0:T(8,128)(2,1)S(1)} all-gather(bf16[1,8,256]{2,1,0:T(8,128)(2,1)S(1)} %get-tuple-element.236), channel_id=15, replica_groups=mesh['clip'=8,'sp'=4] {'clip','sp'}, dimensions={1}, use_global_device_ids=true | all-gather | bytes 135168 | tf_op jit(solution)/shard_map/all_gather | solution.py:115
  664.3 41.2 %psum.171 = f32[256]{0:T(256)S(1)} all-reduce(f32[256]{0:T(256)S(1)} %multiply_reduce_fusion.14), channel_id=1, replica_groups=mesh['clip'=8,'sp'=4] {'clip','sp'}, use_global_device_ids=true, to_apply=%region_8.9 | all-reduce | flops 256 | bytes 2048 | tf_op jit(solution)/shard_map/psum | solution.py:35
  716.4 39.7 %psum.172 = f32[1024]{0:T(1024)S(1)} all-reduce(f32[1024]{0:T(1024)S(1)} %get-tuple-element.250), channel_id=1, replica_groups=mesh['clip'=8,'sp'=4] {'clip','sp'}, use_global_device_ids=true, to_apply=%region_10.11 | all-reduce | flops 1024 | bytes 8192 | tf_op jit(solution)/shard_map/psum | solution.py:32
  763.6 40.5 %psum.173 = f32[1024]{0:T(1024)S(1)} all-reduce(f32[1024]{0:T(1024)S(1)} %multiply_reduce_fusion.4), channel_id=1, replica_groups=mesh['clip'=8,'sp'=4] {'clip','sp'}, use_global_device_ids=true, to_apply=%region_12.13 | all-reduce | flops 1024 | bytes 8192 | tf_op jit(solution)/shard_map/psum | solution.py:35
  820.8 39.5 %psum.174 = f32[256]{0:T(256)S(1)} all-reduce(f32[256]{0:T(256)S(1)} %get-tuple-element.252), channel_id=1, replica_groups=mesh['clip'=8,'sp'=4] {'clip','sp'}, use_global_device_ids=true, to_apply=%region_14.15 | all-reduce | flops 256 | bytes 2048 | tf_op jit(solution)/shard_map/psum | solution.py:32
  863.1 40.5 %psum.175 = f32[256]{0:T(256)S(1)} all-reduce(f32[256]{0:T(256)S(1)} %multiply_reduce_fusion.12), channel_id=1, replica_groups=mesh['clip'=8,'sp'=4] {'clip','sp'}, use_global_device_ids=true, to_apply=%region_16.17 | all-reduce | flops 256 | bytes 2048 | tf_op jit(solution)/shard_map/psum | solution.py:35
  911.8 47.9 %all-gather.14 = bf16[1,256,1024]{2,1,0:T(8,128)(2,1)} all-gather(bf16[1,8,1024]{2,1,0:T(8,128)(2,1)S(1)} %copy-done.38), channel_id=16, replica_groups=mesh['clip'=8,'sp'=4] {'clip','sp'}, dimensions={1}, use_global_device_ids=true | all-gather | bytes 540672 | tf_op jit(solution)/shard_map/all_gather | solution.py:116
  1019.8 41.6 %psum.177 = f32[256]{0:T(256)} all-reduce(f32[256]{0:T(256)} %multiply_reduce_fusion.10), channel_id=1, replica_groups=mesh['clip'=8,'sp'=4] {'clip','sp'}, use_global_device_ids=true, to_apply=%region_20.21 | all-reduce | flops 256 | bytes 2048 | tf_op jit(solution)/shard_map/psum | solution.py:35
  1073.8 40.0 %psum.178 = f32[1024]{0:T(1024)} all-reduce(f32[1024]{0:T(1024)} %get-tuple-element.254), channel_id=1, replica_groups=mesh['clip'=8,'sp'=4] {'clip','sp'}, use_global_device_ids=true, to_apply=%region_22.23 | all-reduce | flops 1024 | bytes 8192 | tf_op jit(solution)/shard_map/psum | solution.py:32
  1122.5 41.4 %psum.179 = f32[1024]{0:T(1024)} all-reduce(f32[1024]{0:T(1024)} %multiply_reduce_fusion.2), channel_id=1, replica_groups=mesh['clip'=8,'sp'=4] {'clip','sp'}, use_global_device_ids=true, to_apply=%region_24.25 | all-reduce | flops 1024 | bytes 8192 | tf_op jit(solution)/shard_map/psum | solution.py:35
  1187.7 40.1 %all-reduce.15 = (f32[1024]{0:T(1024)}, f32[1024]{0:T(1024)}) all-reduce(f32[1024]{0:T(1024)} %get-tuple-element.53, f32[1024]{0:T(1024)} %get-tuple-element.52), channel_id=1, replica_groups=mesh['clip'=8,'sp'=4] {'clip','sp'}, use_global_device_ids=true, to_apply=%region_28.29 | all-reduce | flops 2048 | bytes 16384 | tf_op jit(solution)/shard_map/psum | solution.py:40
  1246.8 41.1 %all-reduce.14 = (f32[256]{0:T(256)}, f32[256]{0:T(256)}) all-reduce(f32[256]{0:T(256)} %get-tuple-element.115, f32[256]{0:T(256)} %get-tuple-element.114), channel_id=1, replica_groups=mesh['clip'=8,'sp'=4] {'clip','sp'}, use_global_device_ids=true, to_apply=%region_32.33 | all-reduce | flops 512 | bytes 4096 | tf_op jit(solution)/shard_map/psum | solution.py:40
  1339.9 42.9 %all-reduce.13 = (f32[256]{0:T(256)S(1)}, f32[256]{0:T(256)S(1)}) all-reduce(f32[256]{0:T(256)S(1)} %get-tuple-element.113, f32[256]{0:T(256)S(1)} %get-tuple-element.112), channel_id=1, replica_groups=mesh['clip'=8,'sp'=4] {'clip','sp'}, use_global_device_ids=true, to_apply=%region_36.37 | all-reduce | flops 512 | bytes 4096 | tf_op jit(solution)/shard_map/psum | solution.py:40
  1408.3 40.5 %all-reduce.12 = (f32[1024]{0:T(1024)S(1)}, f32[1024]{0:T(1024)S(1)}) all-reduce(f32[1024]{0:T(1024)S(1)} %get-tuple-element.51, f32[1024]{0:T(1024)S(1)} %get-tuple-element.50), channel_id=1, replica_groups=mesh['clip'=8,'sp'=4] {'clip','sp'}, use_global_device_ids=true, to_apply=%region_40.41 | all-reduce | flops 2048 | bytes 16384 | tf_op jit(solution)/shard_map/psum | solution.py:40
  1467.1 39.9 %all-reduce.11 = (f32[256]{0:T(256)}, f32[256]{0:T(256)}) all-reduce(f32[256]{0:T(256)} %get-tuple-element.111, f32[256]{0:T(256)} %get-tuple-element.110), channel_id=1, replica_groups=mesh['clip'=8,'sp'=4] {'clip','sp'}, use_global_device_ids=true, to_apply=%region_44.45 | all-reduce | flops 512 | bytes 4096 | tf_op jit(solution)/shard_map/psum | solution.py:40
  1615.9 43.9 %all-reduce.10 = (f32[256]{0:T(256)S(1)}, f32[256]{0:T(256)S(1)}, f32[27,256]{1,0:T(8,128)S(1)}, f32[27,256]{1,0:T(8,128)S(1)}) all-reduce(f32[256]{0:T(256)S(1)} %get-tuple-element.109, f32[256]{0:T(256)S(1)} %get-tuple-element.108, f32[27,256]{1,0:T(8,128)S(1)} %copy-done.37, ...), channel_id=1, replica_groups=mesh['clip'=8,'sp'=4] {'clip','sp'}, use_global_device_ids=true, to_apply=%region_48.49 | all-reduce | flops 14336 | bytes 114688 | tf_op jit(solution)/shard_map/psum | solution.py:40
  1697.0 98.9 %reduce-scatter.13.cloned.1.call-done = f32[8,256]{1,0:T(8,128)} async-done(((f32[256,256]{1,0:T(8,128)}), f32[8,256]{1,0:T(8,128)}) %reduce-scatter.13.cloned.1.call-update) | async-done | bytes 8208 | tf_op jit(solution)/shard_map/reduce_scatter | solution.py:237
  1797.2 131.6 %reduce-scatter.23.cloned.1.call-done = f32[32,256]{1,0:T(8,128)} async-done(((f32[1024,256]{1,0:T(8,128)}), f32[32,256]{1,0:T(8,128)}) %reduce-scatter.23.cloned.1.call-update) | async-done | bytes 32784
  1929.8 132.0 %reduce-scatter.19.cloned.1.call-done = f32[8,1024]{1,0:T(8,128)} async-done(((f32[256,1024]{1,0:T(8,128)}), f32[8,1024]{1,0:T(8,128)}) %reduce-scatter.19.cloned.1.call-update) | async-done | bytes 32784 | tf_op jit(solution)/shard_map/reduce_scatter | solution.py:238
  2061.8 132.8 %reduce-scatter.17.cloned.1.call-done = f32[8,1024]{1,0:T(8,128)} async-done(((f32[256,1024]{1,0:T(8,128)}), f32[8,1024]{1,0:T(8,128)}) %reduce-scatter.17.cloned.1.call-update) | async-done | bytes 32784 | tf_op jit(solution)/shard_map/reduce_scatter | solution.py:238
  2196.0 131.5 %reduce-scatter.21.cloned.1.call-done = f32[32,256]{1,0:T(8,128)} async-done(((f32[1024,256]{1,0:T(8,128)}), f32[32,256]{1,0:T(8,128)}) %reduce-scatter.21.cloned.1.call-update) | async-done | bytes 32784
  (547 shorter events, 900.7 us)
Async XLA Ops:
  7.2 1689.9 %reduce-scatter.15.cloned.1.call-start = ((), (), s32[]{:S(2)}) async-start(), calls=%async_computation.7 | async-start | bytes 270336 | tf_op jit(solution)/shard_map/reduce_scatter | solution.py:237
  60.3 209.4 %copy-start.118 = (f32[256]{0:T(256)}, f32[256]{0:T(256)S(1)}, u32[]{:S(2)}) copy-start(f32[256]{0:T(256)S(1)} %get-tuple-element.154) | copy-start | bytes 3076
  101.5 168.1 %copy-start.162 = (f32[256]{0:T(256)}, f32[256]{0:T(256)S(1)}, u32[]{:S(2)}) copy-start(f32[256]{0:T(256)S(1)} %get-tuple-element.156) | copy-start | bytes 3076
  139.8 133.1 %copy-start.31 = (bf16[1,256,256]{2,1,0:T(8,128)(2,1)}, bf16[1,256,256]{2,1,0:T(8,128)(2,1)S(1)}, u32[]{:S(2)}) copy-start(bf16[1,256,256]{2,1,0:T(8,128)(2,1)S(1)} %all-gather.5) | copy-start | bytes 393220
  273.7 335.3 %copy-start.5 = (bf16[4,4,7,28,256]{4,3,2,1,0:T(8,128)(2,1)}, bf16[4,4,7,28,256]{4,3,2,1,0:T(8,128)(2,1)S(1)}, u32[]{:S(2)}) copy-start(bf16[4,4,7,28,256]{4,3,2,1,0:T(8,128)(2,1)S(1)} %convolution_convert_fusion.1) | copy-start | bytes 4816900
  274.6 330.6 %collective-permute-start = (bf16[4,4,1,28,256]{4,3,2,1,0:T(8,128)(2,1)}, bf16[4,4,1,28,256]{4,3,2,1,0:T(8,128)(2,1)S(1)}, u32[]{:S(2)}, u32[]{:S(2)}) collective-permute-start(bf16[4,4,1,28,256]{4,3,2,1,0:T(8,128)(2,1)} %get-tuple-element.230), channel_id=1, source_target_pairs={{0,1},{1,2},{2,3},{4,5},{5,6},{6,7},{8,9},{9,10},{10,11},{12,13},{... | collective-permute-start | bytes 688136 | tf_op jit(solution)/shard_map/ppermute | solution.py:16
  275.9 329.3 %collective-permute-start.1 = (bf16[4,4,1,28,256]{4,3,2,1,0:T(8,128)(2,1)}, bf16[4,4,1,28,256]{4,3,2,1,0:T(8,128)(2,1)S(1)}, u32[]{:S(2)}, u32[]{:S(2)}) collective-permute-start(bf16[4,4,1,28,256]{4,3,2,1,0:T(8,128)(2,1)} %get-tuple-element.231), channel_id=1, source_target_pairs={{1,0},{2,1},{3,2},{5,4},{6,5},{7,6},{9,8},{10,9},{11,10},{13,12},{... | collective-permute-start | bytes 688136 | tf_op jit(solution)/shard_map/ppermute | solution.py:17
  362.9 246.0 %copy-start.57 = (f32[256]{0:T(256)}, f32[256]{0:T(256)S(1)}, u32[]{:S(2)}) copy-start(f32[256]{0:T(256)S(1)} %get-tuple-element.157) | copy-start | bytes 3076
  401.7 403.0 %copy-start.45 = (f32[1024]{0:T(1024)}, f32[1024]{0:T(1024)S(1)}, u32[]{:S(2)}) copy-start(f32[1024]{0:T(1024)S(1)} %convert_element_type.640) | copy-start | bytes 12292
  445.2 462.9 %copy-start.32 = (bf16[1,256,256]{2,1,0:T(8,128)(2,1)}, bf16[1,256,256]{2,1,0:T(8,128)(2,1)S(1)}, u32[]{:S(2)}) copy-start(bf16[1,256,256]{2,1,0:T(8,128)(2,1)S(1)} %all-gather.13) | copy-start | bytes 393220
  565.8 248.6 %copy-start.28 = (bf16[1,1024,256]{2,1,0:T(8,128)(2,1)}, bf16[1,1024,256]{2,1,0:T(8,128)(2,1)S(1)}, u32[]{:S(2)}) copy-start(bf16[1,1024,256]{2,1,0:T(8,128)(2,1)S(1)} %all-gather.11) | copy-start | bytes 1572868
  605.2 100.9 %copy-start.34 = (bf16[1,256,1024]{2,1,0:T(8,128)(2,1)}, bf16[1,256,1024]{2,1,0:T(8,128)(2,1)S(1)}, u32[]{:S(2)}) copy-start(bf16[1,256,1024]{2,1,0:T(8,128)(2,1)S(1)} %all-gather.6) | copy-start | bytes 1572868
  909.1 50.7 %collective-permute-start.2 = (bf16[4,4,1,28,256]{4,3,2,1,0:T(8,128)(2,1)S(1)}, bf16[4,4,1,28,256]{4,3,2,1,0:T(8,128)(2,1)S(1)}, u32[]{:S(2)}, u32[]{:S(2)}) collective-permute-start(bf16[4,4,1,28,256]{4,3,2,1,0:T(8,128)(2,1)S(1)} %get-tuple-element.228), channel_id=1, source_target_pairs={{0,1},{1,2},{2,3},{4,5},{5,6},{6,7},{8,9},{9,10},{10,11},{12,13},{... | collective-permute-start | bytes 688136 | tf_op jit(solution)/shard_map/ppermute | solution.py:16
  910.5 49.2 %collective-permute-start.3 = (bf16[4,4,1,28,256]{4,3,2,1,0:T(8,128)(2,1)S(1)}, bf16[4,4,1,28,256]{4,3,2,1,0:T(8,128)(2,1)S(1)}, u32[]{:S(2)}, u32[]{:S(2)}) collective-permute-start(bf16[4,4,1,28,256]{4,3,2,1,0:T(8,128)(2,1)S(1)} %get-tuple-element.229), channel_id=1, source_target_pairs={{1,0},{2,1},{3,2},{5,4},{6,5},{7,6},{9,8},{10,9},{11,10},{13,12},{... | collective-permute-start | bytes 688136 | tf_op jit(solution)/shard_map/ppermute | solution.py:17
  963.4 325.8 %copy-start.2 = (bf16[4,6,9,30,256]{4,3,2,1,0:T(8,128)(2,1)}, bf16[4,6,9,30,256]{4,3,2,1,0:T(8,128)(2,1)S(1)}, u32[]{:S(2)}) copy-start(bf16[4,6,9,30,256]{4,3,2,1,0:T(8,128)(2,1)S(1)} %select_maximum_fusion.4) | copy-start | bytes 9953284
  1303.4 15.0 collective-permute-start.4
  1304.8 13.7 collective-permute-start.5
  1523.5 5.2 collective-permute-start.6
  1525.5 5.8 collective-permute-start.7
  1528.2 267.7 %reduce-scatter.13.cloned.1.call-start = ((), (), s32[]{:S(2)}) async-start(), calls=%async_computation.6 | async-start | bytes 270336 | tf_op jit(solution)/shard_map/reduce_scatter | solution.py:237
  1552.2 376.6 %reduce-scatter.23.cloned.1.call-start = ((), (), s32[]{:S(2)}) async-start(), calls=%async_computation.11 | async-start | bytes 1081344
  1561.1 500.7 %reduce-scatter.19.cloned.1.call-start = ((), (), s32[]{:S(2)}) async-start(), calls=%async_computation.9 | async-start | bytes 1081344 | tf_op jit(solution)/shard_map/reduce_scatter | solution.py:238
  1570.0 624.5 %reduce-scatter.17.cloned.1.call-start = ((), (), s32[]{:S(2)}) async-start(), calls=%async_computation.8 | async-start | bytes 1081344 | tf_op jit(solution)/shard_map/reduce_scatter | solution.py:238
  1596.9 730.6 %reduce-scatter.21.cloned.1.call-start = ((), (), s32[]{:S(2)}) async-start(), calls=%async_computation.10 | async-start | bytes 1081344
  (174 other events, 5836.2 us)
Sparse Core Ops, SparseCore 0:
  1528.4 135.8 reduce-scatter.14
  1666.5 129.3 reduce-scatter.12
  1798.1 130.6 reduce-scatter.22
  1931.0 130.7 reduce-scatter.18
  2063.9 130.6 reduce-scatter.16
  2196.8 130.7 reduce-scatter.20
where the time goes:
time: 2350 us; the launch traced here: 2340 us
  blocking collectives  1240 us (53%)
  waiting for transfers between devices  630 us (27%)
  other arithmetic  238 us (10%)
  matrix products  123 us (5%)
  local copies, waits for them, and re-layouts  72.6 us (3%)
    reduce_scatter x2, waiting for transfers between devices, backward_block(): lax.psum_scatter(grad_third, ('clip', 'sp'), scatter_dimension=0, tiled=T...  265 us
    unnamed x8, waiting for transfers between devices  263 us
    psum x6, blocking collectives, norm_back(): lax.psum((channel_sum(upstream), channel_sum(upstream * normed)), ('clip'...  248 us
    psum x6, blocking collectives, moments(): lax.psum(channel_sum(center * center * valid_mask), ('clip', 'sp'))  248 us
    psum x6, blocking collectives, moments(): amount = lax.psum(channel_sum(source * valid_mask), ('clip', 'sp'))  230 us
    reduce_sum x13, other arithmetic, channel_sum(): return jnp.sum(source, axis=(0, 1, 2, 3))  124 us
    reduce_scatter x2, waiting for transfers between devices, backward_block(): lax.psum_scatter(grad_second, ('clip', 'sp'), scatter_dimension=0, tiled=...  98.9 us
    all_gather x2, blocking collectives, fetch_forward(): lax.all_gather(params[2][layer], ('clip', 'sp'), axis=0, tiled=True)  87.3 us
  transfers between devices with their start and end apart: 14, of which 6 were waited for; matrix products, arithmetic and copies ran while one was open for 7% of the time, Pallas kernels for 0%

commit v1 on v0

v1 whole, which is shorter than its diff:
```python
import functools

import jax
import jax.numpy as jnp
from jax import lax
from jax.experimental import pallas as pl
from jax.experimental.pallas import tpu as pltpu
from jax.sharding import Mesh, PartitionSpec as P

epsilon = 1e-05
F32 = jnp.float32
BF16 = jnp.bfloat16
LINE = 32


def dot_nn(left, right):
    return lax.dot_general(left, right, (((1,), (0,)), ((), ())), preferred_element_type=F32)


def dot_nt(left, right):
    return lax.dot_general(left, right, (((1,), (1,)), ((), ())), preferred_element_type=F32)


def dot_tn(left, right):
    return lax.dot_general(left, right, (((0,), (0,)), ((), ())), preferred_element_type=F32)


def dot_split(left, right):
    high = left.astype(BF16)
    rest = (left - high.astype(F32)).astype(BF16)
    return dot_nn(high, right) + dot_nn(rest, right)


def sigmoid(value):
    return 0.5 * jnp.tanh(0.5 * value) + 0.5


def fold(value):
    return jnp.sum(value.reshape(-1, 8, value.shape[-1]), axis=0)


def column_mask(columns):
    return lax.broadcasted_iota(jnp.int32, (LINE, 1), 0) < columns


def full(shape):
    return pl.BlockSpec(shape, lambda *_: (0,) * len(shape))


def smem():
    return pl.BlockSpec(memory_space=pltpu.SMEM)


def call(body, grid, in_specs, out_specs, out_shape, scratch, flops=0, moved=0):
    return pl.pallas_call(
        body,
        grid=grid,
        in_specs=in_specs,
        out_specs=out_specs,
        out_shape=out_shape,
        scratch_shapes=scratch,
        compiler_params=pltpu.CompilerParams(
            dimension_semantics=("arbitrary",) * len(grid), vmem_limit_bytes=58 * 2**20
        ),
    )


def merge_stats(means, squares, counts, total):
    mean = jnp.sum(means * counts, axis=0) / total
    away = means - mean[None]
    spread = jnp.sum(squares + counts * away * away, axis=0) / total
    return mean, lax.rsqrt(spread + epsilon)


def depth_tile(read, weights, frame, frames, flip):
    sums = [None, None, None]
    for a in range(3):
        other = frame + a - 1
        if other < 0 or other >= frames:
            continue
        for b in range(3):
            row = read(other, b).reshape(LINE // 8, 8, -1)
            for e in range(3):
                tap = 9 * a + 3 * b + e
                term = row * weights(26 - tap if flip else tap)[None]
                sums[e] = term if sums[e] is None else sums[e] + term
    first, middle, last = (one.reshape(LINE, -1) for one in sums)
    return pltpu.roll(first, 1, 0) + middle + pltpu.roll(last, LINE - 1, 0)


def first_kernel(dims, scal, nf, x_ref, w_ref, red_ref, up_ref, dn_ref, st_ref, xs, acc):
    frames, rows, columns, group = dims
    clip, part = pl.program_id(0), pl.program_id(1)

    @pl.when((clip == 0) & (part == 0))
    def _():
        xs[...] = jnp.zeros_like(xs)
        acc[...] = jnp.zeros_like(acc)

    for f in range(group):
        live = part * group + f < scal[clip]

        @pl.when(live)
        def _():
            for r in range(rows):
                xs[r, 0:columns, :] = x_ref[0, f, r]
            reduced_tail(dims, f, clip, part, xs, w_ref, red_ref, up_ref, dn_ref, acc)

        @pl.when(jnp.logical_not(live))
        def _():
            red_ref[0, f] = jnp.zeros_like(red_ref[0, f])
            up_ref[0, f] = jnp.zeros_like(up_ref[0, f])
            dn_ref[0, f] = jnp.zeros_like(dn_ref[0, f])

    finish_stats(nf, acc, st_ref)


def reduced_tail(dims, f, clip, part, xs, w_ref, red_ref, up_ref, dn_ref, acc):
    frames, rows, columns, group = dims
    red = dot_nn(xs[...].reshape(rows * LINE, -1), w_ref[...])
    red_ref[0, f] = red.reshape(rows, LINE, -1)
    up_ref[0, f] = red_ref[0, f, 0]
    dn_ref[0, f] = red_ref[0, f, rows - 1]

    if f == 0:

        @pl.when((clip == 0) & (part == 0))
        def _():
            acc[0:1, :] = jnp.sum(red, axis=0, keepdims=True) / (rows * columns)

    collect_stats(rows, columns, lambda r: red_ref[0, f, r], acc)


def collect_stats(rows, columns, read, acc):
    pivot = acc[0:1, :]
    mask = column_mask(columns)

    def one(r, carry):
        plain, square = carry
        away = jnp.where(mask, read(r) - pivot, 0.0)
        return plain + fold(away), square + fold(away * away)

    zero = jnp.zeros((8, acc.shape[1]), F32)
    plain, square = lax.fori_loop(0, rows, one, (zero, zero), unroll=True)
    acc[1:2, :] += jnp.sum(plain, axis=0, keepdims=True)
    acc[2:3, :] += jnp.sum(square, axis=0, keepdims=True)


def finish_stats(nf, acc, st_ref):
    plain, square = acc[1:2, :], acc[2:3, :]
    width = acc.shape[1]
    st_ref[:, 0:width] = acc[0:1, :] + plain * nf[2]
    st_ref[:, width:] = square - plain * plain * nf[2]


def mix_kernel(
    dims, layer, scal, nf, red_ref, up_ref, dn_ref, got_ref, cnt_ref, par_ref, w_ref,
    mix_ref, spa_ref, z_ref, u_ref, h_ref, st_ref, vec_ref, hs, ms, wb, acc,
):
    frames, rows, columns = dims
    clip, clips = pl.program_id(0), pl.num_programs(0)
    width = w_ref.shape[0]
    mask = column_mask(columns)

    @pl.when(clip == 0)
    def _():
        mean, inverse = merge_stats(
            got_ref[:, :, 0:width], got_ref[:, :, width:], cnt_ref[:, :, 0:1], nf[1]
        )
        gain = par_ref[54 + 2 * layer : 55 + 2 * layer, :]
        vec_ref[...] = jnp.zeros_like(vec_ref)
        vec_ref[0:1, :] = inverse
        vec_ref[1:2, :] = -mean * inverse
        vec_ref[2:3, :] = gain
        vec_ref[3:4, :] = par_ref[58 + 2 * layer : 59 + 2 * layer, :]
        vec_ref[4:5, :] = gain * inverse
        acc[...] = jnp.zeros_like(acc)
        hs[...] = jnp.zeros_like(hs)
        for tap in range(27):
            row = par_ref[27 * layer + tap : 27 * layer + tap + 1, :]
            wb[tap] = jnp.broadcast_to(row, (8, width))

    inverse, shift = vec_ref[0:1, :], vec_ref[1:2, :]
    gain, bias = vec_ref[2:3, :], vec_ref[3:4, :]

    def activate(value, keep):
        z = jnp.where(mask, value * inverse + shift, 0.0)
        y = z * gain + bias
        s = sigmoid(y)
        h = jnp.where(keep, y * s, 0.0)
        return z, s, h

    for f in range(frames):
        live = f < scal[clip]

        @pl.when(live)
        def _():
            _, _, h = activate(up_ref[0, f], mask & (scal[clips] > 0))
            hs[f, 0] = h.astype(BF16)
            _, _, h = activate(dn_ref[0, f], mask & (scal[clips + 1] > 0))
            hs[f, rows + 1] = h.astype(BF16)

            def one(r, _):
                z, s, h = activate(red_ref[0, f, r], mask)
                low = h.astype(BF16)
                hs[f, r + 1] = low
                h_ref[0, f, r] = low
                z_ref[0, f, r] = z.astype(BF16)
                u_ref[0, f, r] = jnp.where(mask, s + h * (1.0 - s), 0.0).astype(BF16)
                return 0

            lax.fori_loop(0, rows, one, 0)
            mixed = dot_nn(hs[f].reshape((rows + 2) * LINE, width), w_ref[...]).astype(BF16)
            mix_ref[0, f] = mixed.reshape(rows + 2, LINE, width)
            ms[f] = mixed.astype(F32).reshape(rows + 2, LINE, width)

        @pl.when(jnp.logical_not(live))
        def _():
            h_ref[0, f] = jnp.zeros_like(h_ref[0, f])
            z_ref[0, f] = jnp.zeros_like(z_ref[0, f])
            u_ref[0, f] = jnp.zeros_like(u_ref[0, f])
            mix_ref[0, f] = jnp.zeros_like(mix_ref[0, f])
            ms[f] = jnp.zeros_like(ms[f])

    for f in range(frames):
        live = f < scal[clip]

        @pl.when(live)
        def _():
            for half in range(width // 128):
                lanes = pl.ds(128 * half, 128)

                def one(r, _):
                    tile = depth_tile(
                        lambda t, b: ms[t, r + b, :, lanes],
                        lambda tap: wb[tap, :, lanes],
                        f, frames, False,
                    )
                    spa_ref[0, f, r, :, lanes] = tile
                    return 0

                lax.fori_loop(0, rows, one, 0)

            if f == 0:

                @pl.when(clip == 0)
                def _():
                    total = jnp.zeros((8, width), F32)
                    for r in range(rows):
                        total += fold(jnp.where(mask, spa_ref[0, f, r], 0.0))
                    acc[0:1, :] = jnp.sum(total, axis=0, keepdims=True) / (rows * columns)

            collect_stats(rows, columns, lambda r: spa_ref[0, f, r], acc)

        @pl.when(jnp.logical_not(live))
        def _():
            spa_ref[0, f] = jnp.zeros_like(spa_ref[0, f])

    finish_stats(nf, acc, st_ref)


def hidden_kernel(
    dims, layer, scal, nf, spa_ref, got_ref, cnt_ref, par_ref, w_ref,
    z_ref, u_ref, h_ref, up_ref, dn_ref, st_ref, gram_ref, vec_ref,
):
    frames, rows, columns = dims
    clip = pl.program_id(0)
    width = par_ref.shape[1]
    mask = column_mask(columns)

    @pl.when(clip == 0)
    def _():
        mean, inverse = merge_stats(
            got_ref[:, :, 0:width], got_ref[:, :, width:], cnt_ref[:, :, 0:1], nf[1]
        )
        gain = par_ref[55 + 2 * layer : 56 + 2 * layer, :]
        vec_ref[...] = jnp.zeros_like(vec_ref)
        vec_ref[0:1, :] = inverse
        vec_ref[1:2, :] = -mean * inverse
        vec_ref[2:3, :] = gain
        vec_ref[3:4, :] = par_ref[59 + 2 * layer : 60 + 2 * layer, :]
        vec_ref[4:5, :] = gain * inverse
        gram_ref[...] = jnp.zeros_like(gram_ref)

    inverse, shift = vec_ref[0:1, :], vec_ref[1:2, :]
    gain, bias = vec_ref[2:3, :], vec_ref[3:4, :]

    for f in range(frames):
        live = f < scal[clip]

        @pl.when(live)
        def _():
            def one(r, _):
                z = jnp.where(mask, spa_ref[0, f, r] * inverse + shift, 0.0)
                y = z * gain + bias
                s = sigmoid(y)
                h = y * s
                h_ref[0, f, r] = jnp.where(mask, h, 0.0).astype(BF16)
                z_ref[0, f, r] = z.astype(BF16)
                u_ref[0, f, r] = jnp.where(mask, s + h * (1.0 - s), 0.0).astype(BF16)
                return 0

            lax.fori_loop(0, rows, one, 0)
            low = h_ref[0, f].reshape(rows * LINE, width)
            gram_ref[0:width, :] += dot_tn(low, low)
            ones = jnp.ones((16, rows * LINE), BF16)
            gram_ref[width : width + 8, :] += dot_nn(ones, low)[0:8]

        @pl.when(jnp.logical_not(live))
        def _():
            h_ref[0, f] = jnp.zeros_like(h_ref[0, f])
            z_ref[0, f] = jnp.zeros_like(z_ref[0, f])
            u_ref[0, f] = jnp.zeros_like(u_ref[0, f])

        up_ref[0, f] = z_ref[0, f, 0]
        dn_ref[0, f] = z_ref[0, f, rows - 1]

    @pl.when(clip == pl.num_programs(0) - 1)
    def _():
        total = gram_ref[width : width + 1, :]
        across = jnp.broadcast_to(total, (width, width))
        centered = gram_ref[0:width, :] - across.T * across * nf[2]
        spread = dot_split(centered, w_ref[...]) * w_ref[...].astype(F32)
        st_ref[:, 0:width] = total
        st_ref[:, width:] = jnp.sum(spread, axis=0, keepdims=True)


def wide_norm(nf, got_ref, cnt_ref, rinv_ref, pout_ref, layer, w_ref, vec_ref):
    width = w_ref.shape[0]
    places = got_ref.shape[0]
    hidden_means = got_ref[:, 0, 0:width] * rinv_ref[:, 0:1]
    means = dot_split(hidden_means, w_ref[...])
    counts = cnt_ref[:, 0, 0:1]
    mean = jnp.sum(means * counts, axis=0, keepdims=True) / nf[1]
    away = means - mean
    spread = jnp.sum(got_ref[:, 0, width:] + counts * away * away, axis=0, keepdims=True) / nf[1]
    inverse = lax.rsqrt(spread + epsilon)
    scale = pout_ref[layer : layer + 1, :] * inverse
    vec_ref[...] = jnp.zeros_like(vec_ref)
    vec_ref[0:1, :] = scale
    vec_ref[1:2, :] = pout_ref[2 + layer : 3 + layer, :] - mean * scale
    vec_ref[2:3, :] = inverse
    vec_ref[3:4, :] = mean


def join_kernel(
    dims, scal, nf, x_ref, h_ref, got_ref, cnt_ref, rinv_ref, pout_ref, w3_ref, w1_ref,
    next_ref, du_ref, red_ref, up_ref, dn_ref, st_ref, vec_ref, es, xs, acc,
):
    frames, rows, columns, group = dims
    clip, part = pl.program_id(0), pl.program_id(1)
    wide = w1_ref.shape[0]

    @pl.when((clip == 0) & (part == 0))
    def _():
        wide_norm(nf, got_ref, cnt_ref, rinv_ref, pout_ref, 0, w3_ref, vec_ref)
        xs[...] = jnp.zeros_like(xs)
        acc[...] = jnp.zeros_like(acc)

    for f in range(group):
        live = part * group + f < scal[clip]

        @pl.when(live)
        def _():
            es[...] = dot_nn(h_ref[0, f].reshape(rows * LINE, -1), w3_ref[...]).reshape(es.shape)

            def one(r, _):
                for j in range(wide // 256):
                    lanes = pl.ds(256 * j, 256)
                    y = x_ref[0, f, r, :, lanes].astype(F32) + (
                        es[r, 0:columns, lanes] * vec_ref[0:1, lanes] + vec_ref[1:2, lanes]
                    )
                    s = sigmoid(y)
                    o = y * s
                    xs[r, 0:columns, lanes] = o.astype(BF16)
                    du_ref[0, f, r, :, lanes] = (s + o * (1.0 - s)).astype(BF16)
                return 0

            lax.fori_loop(0, rows, one, 0)
            next_ref[0, f] = xs[...]
            reduced_tail(dims, f, clip, part, xs, w1_ref, red_ref, up_ref, dn_ref, acc)

        @pl.when(jnp.logical_not(live))
        def _():
            next_ref[0, f] = jnp.zeros_like(next_ref[0, f])
            du_ref[0, f] = jnp.zeros_like(du_ref[0, f])
            red_ref[0, f] = jnp.zeros_like(red_ref[0, f])
            up_ref[0, f] = jnp.zeros_like(up_ref[0, f])
            dn_ref[0, f] = jnp.zeros_like(dn_ref[0, f])

    finish_stats(nf, acc, st_ref)


def wide_tail(f, rows, h_ref, gs, w3s, low_ref, t_ref, ones_rows):
    low = h_ref[0, f].reshape(rows * LINE, -1)
    grad = gs[...].reshape(rows * LINE, -1)
    width = low.shape[1]
    t_ref[0:width, :] += dot_tn(low, grad)
    t_ref[width : width + 8, :] += dot_nn(ones_rows, grad)[0:8]
    low_ref[0, f] = dot_nt(grad, w3s[...]).reshape(rows, LINE, width)


def wide_sums(w3_ref, t_ref, vec_ref, sum_ref):
    width, wide = w3_ref.shape
    plain = t_ref[width : width + 1, :]
    along = jnp.sum(w3_ref[...].astype(F32) * t_ref[0:width, :], axis=0, keepdims=True)
    sum_ref[:, 0:wide] = plain
    sum_ref[:, wide:] = (along - vec_ref[3:4, :] * plain) * vec_ref[2:3, :]


def out_kernel(
    dims, scal, nf, x_ref, h_ref, cot_ref, got_ref, cnt_ref, rinv_ref, pout_ref, w3_ref,
    out_ref, gs_ref, low_ref, t_ref, sum_ref, vec_ref, es, gs, w3s,
):
    frames, rows, columns, group = dims
    clip, part = pl.program_id(0), pl.program_id(1)
    width, wide = w3_ref.shape

    @pl.when((clip == 0) & (part == 0))
    def _():
        wide_norm(nf, got_ref, cnt_ref, rinv_ref, pout_ref, 1, w3_ref, vec_ref)
        gs[...] = jnp.zeros_like(gs)
        t_ref[...] = jnp.zeros_like(t_ref)
        w3s[...] = (w3_ref[...].astype(F32) * vec_ref[0:1, :]).astype(BF16)

    for f in range(group):
        live = part * group + f < scal[clip]

        @pl.when(live)
        def _():
            es[...] = dot_nn(h_ref[0, f].reshape(rows * LINE, -1), w3_ref[...]).reshape(es.shape)

            def one(r, _):
                for j in range(wide // 256):
                    lanes = pl.ds(256 * j, 256)
                    y = x_ref[0, f, r, 0:columns, lanes].astype(F32) + (
                        es[r, 0:columns, lanes] * vec_ref[0:1, lanes] + vec_ref[1:2, lanes]
                    )
                    s = sigmoid(y)
                    o = y * s
                    out_ref[0, f, r, :, lanes] = o.astype(BF16)
                    grad = cot_ref[0, f, r, :, lanes].astype(F32) * (s + o * (1.0 - s))
                    grad = grad.astype(BF16)
                    gs[r, 0:columns, lanes] = grad
                    gs_ref[0, f, r, :, lanes] = grad
                return 0

            lax.fori_loop(0, rows, one, 0)
            wide_tail(f, rows, h_ref, gs, w3s, low_ref, t_ref, jnp.ones((16, rows * LINE), BF16))

        @pl.when(jnp.logical_not(live))
        def _():
            out_ref[0, f] = jnp.zeros_like(out_ref[0, f])
            gs_ref[0, f] = jnp.zeros_like(gs_ref[0, f])
            low_ref[0, f] = jnp.zeros_like(low_ref[0, f])

    @pl.when((clip == pl.num_programs(0) - 1) & (part == pl.num_programs(1) - 1))
    def _():
        wide_sums(w3_ref, t_ref, vec_ref, sum_ref)


def expand_back_kernel(
    dims, scal, nf, low_ref, h_ref, z_ref, u_ref, got_ref, vec_ref, t_ref, gram_ref, w3_ref,
    go_ref, up_ref, dn_ref, sum_ref, ge_ref, tot_ref, ks, crow, hk, acc,
):
    frames, rows, columns = dims
    clip = pl.program_id(0)
    width, wide = w3_ref.shape

    @pl.when(clip == 0)
    def _():
        totals = jnp.sum(got_ref[...].astype(F32), axis=0)
        tot_ref[...] = totals
        plain, along = totals[:, 0:wide] * nf[3], totals[:, wide:] * nf[3]
        scale, inverse, mean = vec_ref[0:1, :], vec_ref[2:3, :], vec_ref[3:4, :]
        w3 = w3_ref[...]
        rise = scale * inverse * along
        flat = scale * plain - rise * mean
        ks[...] = dot_nt((w3.astype(F32) * rise).astype(BF16), w3).astype(BF16)
        flat_high = flat.astype(BF16)
        flat_rest = (flat - flat_high.astype(F32)).astype(BF16)
        spread = lambda one: jnp.broadcast_to(one, (16, wide))
        crow[...] = (dot_nt(spread(flat_high), w3) + dot_nt(spread(flat_rest), w3))[0:8]
        total = gram_ref[width : width + 1, :]
        column = jnp.broadcast_to(total, (128, width)).T[:, 0:1]
        cross = dot_split(gram_ref[0:width, :], w3)
        ge = t_ref[0:width, :] * scale - column * flat - cross * rise
        ge_ref[...] = ge.astype(BF16)
        acc[...] = jnp.zeros_like(acc)

    row = crow[0:1, :]
    for f in range(frames):
        live = f < scal[clip]

        @pl.when(live)
        def _():
            hk[...] = dot_nn(h_ref[0, f].reshape(rows * LINE, width), ks[...]).reshape(hk.shape)

            def one(r, carry):
                plain, along = carry
                grad = low_ref[0, f, r] - row - hk[r]
                grad = grad * u_ref[0, f, r].astype(F32)
                go_ref[0, f, r] = grad.astype(BF16)
                z = z_ref[0, f, r].astype(F32)
                return plain + fold(grad), along + fold(grad * z)

            zero = jnp.zeros((8, width), F32)
            plain, along = lax.fori_loop(0, rows, one, (zero, zero))
            acc[0:8, :] += plain
            acc[8:16, :] += along

        @pl.when(jnp.logical_not(live))
        def _():
            go_ref[0, f] = jnp.zeros_like(go_ref[0, f])

        up_ref[0, f] = go_ref[0, f, 0]
        dn_ref[0, f] = go_ref[0, f, rows - 1]

    sum_ref[:, 0:width] = jnp.sum(acc[0:8, :], axis=0, keepdims=True)
    sum_ref[:, width:] = jnp.sum(acc[8:16, :], axis=0, keepdims=True)


def norm_rows(nf, got_ref, vec_ref, tot_ref, rows3):
    width = vec_ref.shape[1]
    totals = jnp.sum(got_ref[...], axis=0)
    tot_ref[...] = totals
    rows3[0:1, :] = vec_ref[4:5, :]
    rows3[1:2, :] = totals[:, 0:width] * nf[3]
    rows3[2:3, :] = totals[:, width:] * nf[3]


def depth_back_kernel(
    dims, layer, scal, nf, go_ref, gup_ref, gdn_ref, z_ref, zup_ref, zdn_ref, got_ref, vec_ref,
    mix_ref, h_ref, z1_ref, u1_ref, par_ref, w_ref,
    go1_ref, sum_ref, gmix_ref, gdep_ref, tot_ref, gp, ms, gm, gh, wb, rows3, gd, acc,
):
    frames, rows, columns = dims
    clip, clips = pl.program_id(0), pl.num_programs(0)
    width = w_ref.shape[0]
    mask = column_mask(columns)

    @pl.when(clip == 0)
    def _():
        norm_rows(nf, got_ref, vec_ref, tot_ref, rows3)
        gmix_ref[...] = jnp.zeros_like(gmix_ref)
        gd[...] = jnp.zeros_like(gd)
        acc[...] = jnp.zeros_like(acc)
        for tap in range(27):
            row = par_ref[27 * layer + tap : 27 * layer + tap + 1, :]
            wb[tap] = jnp.broadcast_to(row, (8, width))

    gain, flat, rise = rows3[0:1, :], rows3[1:2, :], rows3[2:3, :]

    def normed(go, z, keep):
        value = gain * (go.astype(F32) - flat - z.astype(F32) * rise)
        return jnp.where(keep, value, 0.0).astype(BF16).astype(F32)

    for f in range(frames):
        live = f < scal[clip]

        @pl.when(live)
        def _():
            gp[f, 0] = normed(gup_ref[0, f], zup_ref[0, f], mask & (scal[clips] > 0))
            gp[f, rows + 1] = normed(gdn_ref[0, f], zdn_ref[0, f], mask & (scal[clips + 1] > 0))

            def one(r, _):
                gp[f, r + 1] = normed(go_ref[0, f, r], z_ref[0, f, r], mask)
                return 0

            lax.fori_loop(0, rows, one, 0)

            def two(r, _):
                ms[f, r] = mix_ref[0, f, r].astype(F32)
                return 0

            lax.fori_loop(0, rows + 2, two, 0)

        @pl.when(jnp.logical_not(live))
        def _():
            gp[f] = jnp.zeros_like(gp[f])
            ms[f] = jnp.zeros_like(ms[f])

    for f in range(frames):
        live = f < scal[clip]

        @pl.when(live)
        def _():
            for half in range(width // 128):
                lanes = pl.ds(128 * half, 128)

                def one(r, _):
                    tile = depth_tile(
                        lambda t, b: gp[t, r + b, :, lanes],
                        lambda tap: wb[tap, :, lanes],
                        f, frames, True,
                    )
                    gm[f, r, :, lanes] = jnp.where(mask, tile, 0.0).astype(BF16)
                    return 0

                lax.fori_loop(0, rows, one, 0)

                taps = [
                    9 * a + 3 * b + e
                    for a in range(3)
                    if 0 <= f + a - 1 < frames
                    for b in range(3)
                    for e in range(3)
                ]

                def two(r, carry):
                    own = gp[f, r + 1, :, lanes]
                    moved = [
                        pltpu.roll(own, LINE - 1, 0).reshape(-1, 8, 128),
                        own.reshape(-1, 8, 128),
                        pltpu.roll(own, 1, 0).reshape(-1, 8, 128),
                    ]
                    result = []
                    rows_read = {}
                    for tap, kept in zip(taps, carry):
                        a, b, e = tap // 9, tap // 3 % 3, tap % 3
                        if (a, b) not in rows_read:
                            rows_read[a, b] = ms[f + a - 1, r + b, :, lanes].reshape(-1, 8, 128)
                        result.append(kept + jnp.sum(moved[e] * rows_read[a, b], axis=0))
                    return tuple(result)

                start = tuple(gd[tap, :, lanes] for tap in taps)
                for tap, kept in zip(taps, lax.fori_loop(0, rows, two, start)):
                    gd[tap, :, lanes] = kept

            grad = gm[f].reshape(rows * LINE, width)
            gmix_ref[...] += dot_tn(h_ref[0, f].reshape(rows * LINE, width), grad)
            gh[...] = dot_nt(grad, w_ref[...]).reshape(gh.shape)

            def three(r, carry):
                plain, along = carry
                value = gh[r] * u1_ref[0, f, r].astype(F32)
                go1_ref[0, f, r] = value.astype(BF16)
                return plain + fold(value), along + fold(value * z1_ref[0, f, r].astype(F32))

            zero = jnp.zeros((8, width), F32)
            plain, along = lax.fori_loop(0, rows, three, (zero, zero))
            acc[0:8, :] += plain
            acc[8:16, :] += along

        @pl.when(jnp.logical_not(live))
        def _():
            go1_ref[0, f] = jnp.zeros_like(go1_ref[0, f])

    sum_ref[:, 0:width] = jnp.sum(acc[0:8, :], axis=0, keepdims=True)
    sum_ref[:, width:] = jnp.sum(acc[8:16, :], axis=0, keepdims=True)

    @pl.when(clip == pl.num_programs(0) - 1)
    def _():
        gdep_ref[...] = jnp.zeros_like(gdep_ref)
        for tap in range(27):
            gdep_ref[tap : tap + 1, :] = jnp.sum(gd[tap], axis=0, keepdims=True)


def reduced_grad(rows, columns, f, go_ref, z_ref, rows3, gr):
    gain, flat, rise = rows3[0:1, :], rows3[1:2, :], rows3[2:3, :]
    mask = column_mask(columns)

    def one(r, _):
        value = go_ref[0, f, r].astype(F32) - flat - z_ref[0, f, r].astype(F32) * rise
        gr[r] = jnp.where(mask, gain * value, 0.0).astype(BF16)
        return 0

    lax.fori_loop(0, rows, one, 0)


def cross_kernel(
    dims, scal, nf, go_ref, z_ref, got_ref, vec1_ref, x_ref, gs_ref, du_ref, h_ref,
    vec3_ref, w1_ref, w3_ref,
    gs0_ref, low_ref, t_ref, sum_ref, gred_ref, tot_ref, gr, ds, gs, w3s, rows3, gacc,
):
    frames, rows, columns, group = dims
    clip, part = pl.program_id(0), pl.program_id(1)
    width, wide = w3_ref.shape

    @pl.when((clip == 0) & (part == 0))
    def _():
        norm_rows(nf, got_ref, vec1_ref, tot_ref, rows3)
        gs[...] = jnp.zeros_like(gs)
        t_ref[...] = jnp.zeros_like(t_ref)
        gacc[...] = jnp.zeros_like(gacc)
        w3s[...] = (w3_ref[...].astype(F32) * vec3_ref[0:1, :]).astype(BF16)

    for f in range(group):
        live = part * group + f < scal[clip]

        @pl.when(live)
        def _():
            reduced_grad(rows, columns, f, go_ref, z_ref, rows3, gr)
            grad = gr[...].reshape(rows * LINE, width)
            gacc[...] += dot_tn(grad, x_ref[0, f].reshape(rows * LINE, wide))
            ds[...] = dot_nt(grad, w1_ref[...]).reshape(ds.shape)

            def one(r, _):
                for j in range(wide // 256):
                    lanes = pl.ds(256 * j, 256)
                    value = gs_ref[0, f, r, :, lanes].astype(F32) + ds[r, 0:columns, lanes]
                    value = (value * du_ref[0, f, r, :, lanes].astype(F32)).astype(BF16)
                    gs[r, 0:columns, lanes] = value
                    gs0_ref[0, f, r, :, lanes] = value
                return 0

            lax.fori_loop(0, rows, one, 0)
            wide_tail(f, rows, h_ref, gs, w3s, low_ref, t_ref, jnp.ones((16, rows * LINE), BF16))

        @pl.when(jnp.logical_not(live))
        def _():
            gs0_ref[0, f] = jnp.zeros_like(gs0_ref[0, f])
            low_ref[0, f] = jnp.zeros_like(low_ref[0, f])

    @pl.when((clip == pl.num_programs(0) - 1) & (part == pl.num_programs(1) - 1))
    def _():
        wide_sums(w3_ref, t_ref, vec3_ref, sum_ref)
        gred_ref[...] = gacc[...].T.astype(BF16)


def last_kernel(
    dims, scal, nf, go_ref, z_ref, got_ref, vec1_ref, x_ref, gs_ref, w1_ref,
    out_ref, gred_ref, tot_ref, gr, ds, xs, rows3, gacc,
):
    frames, rows, columns, group = dims
    clip, part = pl.program_id(0), pl.program_id(1)
    wide, width = w1_ref.shape

    @pl.when((clip == 0) & (part == 0))
    def _():
        norm_rows(nf, got_ref, vec1_ref, tot_ref, rows3)
        xs[...] = jnp.zeros_like(xs)
        gacc[...] = jnp.zeros_like(gacc)

    for f in range(group):
        live = part * group + f < scal[clip]

        @pl.when(live)
        def _():
            reduced_grad(rows, columns, f, go_ref, z_ref, rows3, gr)
            for r in range(rows):
                xs[r, 0:columns, :] = x_ref[0, f, r]
            grad = gr[...].reshape(rows * LINE, width)
            gacc[...] += dot_tn(grad, xs[...].reshape(rows * LINE, wide))
            ds[...] = dot_nt(grad, w1_ref[...]).reshape(ds.shape)

            def one(r, _):
                for j in range(wide // 256):
                    lanes = pl.ds(256 * j, 256)
                    value = gs_ref[0, f, r, :, lanes].astype(F32) + ds[r, 0:columns, lanes]
                    out_ref[0, f, r, :, lanes] = value.astype(BF16)
                return 0

            lax.fori_loop(0, rows, one, 0)

        @pl.when(jnp.logical_not(live))
        def _():
            out_ref[0, f] = jnp.zeros_like(out_ref[0, f])

    @pl.when((clip == pl.num_programs(0) - 1) & (part == pl.num_programs(1) - 1))
    def _():
        gred_ref[...] = gacc[...].T.astype(BF16)


ALL = ("clip", "outer", "inner")
CHIPS = ("clip", "outer")
SP = ("outer", "inner")


def share(row):
    peers = lax.axis_size(ALL)
    return lax.all_to_all(jnp.broadcast_to(row[None], (peers,) + row.shape), ALL, 0, 0)


def neighbours(from_top, from_bottom):
    peers = lax.axis_size(SP)
    down = [(i, i + 1) for i in range(peers - 1)]
    above = lax.ppermute(from_bottom, SP, down)
    below = lax.ppermute(from_top, SP, [(j, i) for i, j in down])
    return above, below


def swap(value):
    peers = lax.axis_size("inner")
    return lax.ppermute(value, "inner", [(i, (i + 1) % peers) for i in range(peers)])


def on_device(
    features, strides, cotangent, w_reduce, w_mix, w_expand, w_depth,
    gains_mid, biases_mid, gains_out, biases_out,
):
    clips, frames, rows, columns, wide = features.shape
    width = w_mix.shape[2]
    peers, chips = lax.axis_size(ALL), lax.axis_size(CHIPS)
    inner = lax.axis_size("inner")
    sp_size = lax.axis_size(SP)
    part, place = lax.axis_index("inner"), lax.axis_index(ALL)
    sp_at = lax.axis_index(SP)

    counts = frames // strides
    by_group = jnp.sum(counts.reshape(-1, clips), axis=1) * (rows * columns)
    by_device = jnp.repeat(by_group, sp_size).astype(F32)
    local = lax.dynamic_slice_in_dim(counts, lax.axis_index("clip") * clips, clips)
    edges = jnp.stack([sp_at > 0, sp_at < sp_size - 1]).astype(jnp.int32)
    scal = jnp.concatenate([local.astype(jnp.int32), edges])
    own = jnp.sum(local).astype(F32) * (rows * columns)
    total = jnp.sum(by_device)
    nf = jnp.stack([own, total, 1.0 / own, 1.0 / total])
    cnt = jnp.broadcast_to(by_device[:, None, None], (peers, 1, 128))
    rinv = jnp.broadcast_to(1.0 / by_device[:, None], (peers, 128))

    r1, r2 = w_reduce.shape[1], w_mix.shape[1]
    r4 = w_depth.shape[2]
    r5 = gains_out.shape[1] // r4
    small = jnp.concatenate(
        [
            w_depth.transpose(2, 0, 1).reshape(r4, -1),
            gains_mid.transpose(2, 0, 1).reshape(r4, -1),
            biases_mid.transpose(2, 0, 1).reshape(r4, -1),
            jnp.zeros((r4, 2), BF16),
            gains_out.reshape(2, r4, r5).transpose(1, 0, 2).reshape(r4, -1),
            biases_out.reshape(2, r4, r5).transpose(1, 0, 2).reshape(r4, -1),
        ],
        axis=1,
    )
    small = jnp.pad(small, ((0, 0), (0, width - small.shape[1])))
    wide_rows = w_expand.reshape(2, r2, wide // width, width).transpose(0, 2, 1, 3)
    packed = jnp.concatenate(
        [
            w_reduce.reshape(-1, width),
            w_mix.reshape(-1, width),
            wide_rows.reshape(-1, width),
            small,
        ],
        axis=0,
    )
    pad = -packed.shape[0] % 16
    packed = jnp.pad(packed, ((0, pad), (0, 0)))
    near = lax.all_to_all(jnp.broadcast_to(packed[None], (chips,) + packed.shape), CHIPS, 0, 0)
    held = [near]
    for _ in range(inner - 1):
        held.append(swap(held[-1]))
    everything = jnp.stack(
        [lax.select_n(lax.rem(part - c + inner, inner), *held) for c in range(inner)], axis=1
    )
    everything = everything.reshape((peers,) + packed.shape)

    w1, w2, w3 = [], [], []
    base = 0
    for layer in range(2):
        w1.append(everything[:, base + layer * r1 : base + (layer + 1) * r1].reshape(-1, width))
    base += 2 * r1
    for layer in range(2):
        w2.append(everything[:, base + layer * r2 : base + (layer + 1) * r2].reshape(-1, width))
    base += 2 * r2
    blocks = wide // width
    for layer in range(2):
        start = base + layer * r2 * blocks
        one = everything[:, start : start + r2 * blocks].reshape(peers, blocks, r2, width)
        w3.append(one.transpose(0, 2, 1, 3).reshape(peers * r2, wide))
    base += 2 * r2 * blocks
    small = everything[:, base : base + r4]
    par = small[:, :, 0:64].reshape(-1, 64).T.astype(F32)
    out_rows = small[:, :, 64 : 64 + 4 * r5].reshape(peers, r4, 4, r5)
    pout = out_rows.transpose(2, 0, 1, 3).reshape(4, wide).astype(F32)

    pad_field = (clips, frames, rows, LINE, width)
    narrow = lambda kind: jax.ShapeDtypeStruct(pad_field, kind)
    edge = lambda kind: jax.ShapeDtypeStruct((clips, frames, LINE, width), kind)
    flat = lambda *shape: jax.ShapeDtypeStruct(shape, F32)
    group = 2 if frames % 2 == 0 else 1
    dims3 = (frames, rows, columns)
    dims4 = (frames, rows, columns, group)
    grid2 = (clips, frames // group)

    def by_clip(*shape):
        return pl.BlockSpec((1,) + shape, lambda c: (c,) + (0,) * len(shape))

    def by_part(*shape):
        return pl.BlockSpec((1, group) + shape, lambda c, p: (c, p) + (0,) * len(shape))

    line = by_part(rows, LINE, width)
    edge_part = by_part(LINE, width)
    clip_field = by_clip(frames, rows, LINE, width)
    clip_tall = by_clip(frames, rows + 2, LINE, width)
    clip_edge = by_clip(frames, LINE, width)
    raw = by_part(rows, columns, wide)
    kept = by_part(rows, LINE, wide)
    raw_shape = jax.ShapeDtypeStruct((clips, frames, rows, columns, wide), BF16)
    kept_shape = jax.ShapeDtypeStruct((clips, frames, rows, LINE, wide), BF16)

    reduced, up, dn, stats = call(
        functools.partial(first_kernel, dims4), grid2,
        [smem(), smem(), raw, full((wide, width))],
        [line, edge_part, edge_part, full((1, 2 * width))],
        [narrow(F32), edge(F32), edge(F32), flat(1, 2 * width)],
        [pltpu.VMEM((rows, LINE, wide), BF16), pltpu.VMEM((8, width), F32)],
    )(scal, nf, features, w1[0])

    stored = []
    for layer in range(2):
        above, below = neighbours(up, dn)
        got = share(stats)
        mixed, spatial, z1, u1, h1, stats, vec1 = call(
            functools.partial(mix_kernel, dims3, layer), (clips,),
            [smem(), smem(), clip_field, clip_edge, clip_edge, full((peers, 1, 2 * width)),
             full((peers, 1, 128)), full((64, width)), full((width, width))],
            [clip_tall, clip_field, clip_field, clip_field, clip_field,
             full((1, 2 * width)), full((8, width))],
            [jax.ShapeDtypeStruct((clips, frames, rows + 2, LINE, width), BF16), narrow(F32),
             narrow(BF16), narrow(BF16), narrow(BF16), flat(1, 2 * width), flat(8, width)],
            [pltpu.VMEM((frames, rows + 2, LINE, width), BF16),
             pltpu.VMEM((frames, rows + 2, LINE, width), F32),
             pltpu.VMEM((27, 8, width), F32), pltpu.VMEM((8, width), F32)],
        )(scal, nf, reduced, above, below, got, cnt, par, w2[layer])
        got = share(stats)
        z2, u2, h2, zup, zdn, stats, gram, vec2 = call(
            functools.partial(hidden_kernel, dims3, layer), (clips,),
            [smem(), smem(), clip_field, full((peers, 1, 2 * width)), full((peers, 1, 128)),
             full((64, width)), full((width, wide))],
            [clip_field, clip_field, clip_field, clip_edge, clip_edge,
             full((1, width + wide)), full((width + 8, width)), full((8, width))],
            [narrow(BF16), narrow(BF16), narrow(BF16), edge(BF16), edge(BF16),
             flat(1, width + wide), flat(width + 8, width), flat(8, width)],
            [],
        )(scal, nf, spatial, got, cnt, par, w3[layer])
        z_halo = neighbours(zup, zdn)
        got = share(stats)
        norm_specs = [full((peers, 1, width + wide)), full((peers, 1, 128)), full((peers, 128)),
                      full((4, wide)), full((width, wide))]
        norm_args = (got, cnt, rinv, pout, w3[layer])
        if layer == 0:
            carried, slope, reduced, up, dn, stats, vec3 = call(
                functools.partial(join_kernel, dims4), grid2,
                [smem(), smem(), raw, line] + norm_specs + [full((wide, width))],
                [kept, raw, line, edge_part, edge_part, full((1, 2 * width)), full((8, wide))],
                [kept_shape, raw_shape, narrow(F32), edge(F32), edge(F32),
                 flat(1, 2 * width), flat(8, wide)],
                [pltpu.VMEM((rows, LINE, wide), F32), pltpu.VMEM((rows, LINE, wide), BF16),
                 pltpu.VMEM((8, width), F32)],
            )(scal, nf, features, h2, *norm_args, w1[1])
        else:
            output, gs, low, t, sums, vec3 = call(
                functools.partial(out_kernel, dims4), grid2,
                [smem(), smem(), kept, line, raw] + norm_specs,
                [raw, raw, line, full((width + 8, wide)), full((1, 2 * wide)), full((8, wide))],
                [raw_shape, raw_shape, narrow(F32), flat(width + 8, wide), flat(1, 2 * wide),
                 flat(8, wide)],
                [pltpu.VMEM((rows, LINE, wide), F32), pltpu.VMEM((rows, LINE, wide), BF16),
                 pltpu.VMEM((width, wide), BF16)],
            )(scal, nf, carried, h2, cotangent, *norm_args)
        stored.append((z1, u1, h1, vec1, mixed, z2, u2, h2, vec2, z_halo, gram, vec3))

    results = [None, None]
    for layer in (1, 0):
        z1, u1, h1, vec1, mixed, z2, u2, h2, vec2, z_halo, gram, vec3 = stored[layer]
        got = share(sums.astype(BF16))
        go2, gup, gdn, sums, g_expand, tot3 = call(
            functools.partial(expand_back_kernel, dims3), (clips,),
            [smem(), smem(), clip_field, clip_field, clip_field, clip_field,
             full((peers, 1, 2 * wide)), full((8, wide)), full((width + 8, wide)),
             full((width + 8, width)), full((width, wide))],
            [clip_field, clip_edge, clip_edge, full((1, 2 * width)), full((width, wide)),
             full((1, 2 * wide))],
            [narrow(BF16), edge(BF16), edge(BF16), flat(1, 2 * width),
             jax.ShapeDtypeStruct((width, wide), BF16), flat(1, 2 * wide)],
            [pltpu.VMEM((width, width), BF16), pltpu.VMEM((8, width), F32),
             pltpu.VMEM((rows, LINE, width), F32), pltpu.VMEM((16, width), F32)],
        )(scal, nf, low, h2, z2, u2, got, vec3, t, gram, w3[layer])
        above, below = neighbours(gup, gdn)
        got = share(sums)
        go1, sums, g_mix, g_depth, tot2 = call(
            functools.partial(depth_back_kernel, dims3, layer), (clips,),
            [smem(), smem(), clip_field, clip_edge, clip_edge, clip_field, clip_edge, clip_edge,
             full((peers, 1, 2 * width)), full((8, width)), clip_tall, clip_field, clip_field,
             clip_field, full((64, width)), full((width, width))],
            [clip_field, full((1, 2 * width)), full((width, width)), full((LINE, width)),
             full((1, 2 * width))],
            [narrow(BF16), flat(1, 2 * width), flat(width, width), flat(LINE, width),
             flat(1, 2 * width)],
            [pltpu.VMEM((frames, rows + 2, LINE, width), F32),
             pltpu.VMEM((frames, rows + 2, LINE, width), F32),
             pltpu.VMEM((frames, rows, LINE, width), BF16),
             pltpu.VMEM((rows, LINE, width), F32),
             pltpu.VMEM((27, 8, width), F32), pltpu.VMEM((8, width), F32),
             pltpu.VMEM((27, 8, width), F32), pltpu.VMEM((16, width), F32)],
        )(scal, nf, go2, above, below, z2, z_halo[0], z_halo[1], got, vec2, mixed, h1, z1, u1,
          par, w2[layer])
        got = share(sums)
        if layer == 1:
            _, _, _, _, _, _, _, h2_0, _, _, _, vec3_0 = stored[0]
            gs, low, t, sums, g_reduce, tot1 = call(
                functools.partial(cross_kernel, dims4), grid2,
                [smem(), smem(), line, line, full((peers, 1, 2 * width)), full((8, width)),
                 kept, raw, raw, line, full((8, wide)), full((wide, width)),
                 full((width, wide))],
                [raw, line, full((width + 8, wide)), full((1, 2 * wide)), full((wide, width)),
                 full((1, 2 * width))],
                [raw_shape, narrow(F32), flat(width + 8, wide), flat(1, 2 * wide),
                 jax.ShapeDtypeStruct((wide, width), BF16), flat(1, 2 * width)],
                [pltpu.VMEM((rows, LINE, width), BF16), pltpu.VMEM((rows, LINE, wide), F32),
                 pltpu.VMEM((rows, LINE, wide), BF16), pltpu.VMEM((width, wide), BF16),
                 pltpu.VMEM((8, width), F32), pltpu.VMEM((width, wide), F32)],
            )(scal, nf, go1, z1, got, vec1, carried, gs, slope, h2_0, vec3_0, w1[1],
              w3[0])
        else:
            input_grad, g_reduce, tot1 = call(
                functools.partial(last_kernel, dims4), grid2,
                [smem(), smem(), line, line, full((peers, 1, 2 * width)), full((8, width)),
                 raw, raw, full((wide, width))],
                [raw, full((wide, width)), full((1, 2 * width))],
                [raw_shape, jax.ShapeDtypeStruct((wide, width), BF16), flat(1, 2 * width)],
                [pltpu.VMEM((rows, LINE, width), BF16), pltpu.VMEM((rows, LINE, wide), F32),
                 pltpu.VMEM((rows, LINE, wide), BF16), pltpu.VMEM((8, width), F32),
                 pltpu.VMEM((width, wide), F32)],
            )(scal, nf, go1, z1, got, vec1, features, gs, w1[0])
        results[layer] = (g_reduce, g_mix, g_expand, g_depth, tot1, tot2, tot3)

    pieces = []
    for layer in range(2):
        g_reduce, g_mix, g_expand, g_depth = results[layer][0:4]
        pieces.append(g_reduce.reshape(peers, -1, width))
        pieces.append(g_mix.astype(BF16).reshape(peers, -1, width))
        one = g_expand.reshape(peers, r2, blocks, width).transpose(0, 2, 1, 3)
        pieces.append(one.reshape(peers, r2 * blocks, width))
        one = g_depth.astype(BF16).T.reshape(peers, r4, LINE)
        pieces.append(jnp.pad(one, ((0, 0), (0, 0), (0, width - LINE))))
    packed = jnp.concatenate(pieces, axis=1).reshape(chips, inner, -1, width)
    sent = lax.dynamic_index_in_dim(packed, lax.rem(part + 1, inner), 1, keepdims=False)
    mine = lax.dynamic_index_in_dim(packed, part, 1, keepdims=False).astype(F32)
    mine = mine + swap(sent).astype(F32)
    got = lax.all_to_all(mine.astype(BF16), CHIPS, 0, 0)
    got = jnp.sum(got.astype(F32), axis=0)
    grads = [[], [], [], []]
    at = 0
    for layer in range(2):
        grads[0].append(got[at : at + r1])
        at += r1
        grads[1].append(got[at : at + r2])
        at += r2
        one = got[at : at + r2 * blocks].reshape(blocks, r2, width)
        grads[2].append(one.transpose(1, 0, 2).reshape(r2, wide))
        at += r2 * blocks
        grads[3].append(got[at : at + r4, 0:27].T)
        at += r4

    def cut(row, size):
        return lax.dynamic_slice_in_dim(row, place * size, size, axis=1)

    mid_sums = jnp.concatenate(
        [
            jnp.concatenate([results[layer][4], results[layer][5]], axis=0).reshape(2, 2, width)
            for layer in range(2)
        ],
        axis=0,
    )
    mid = lax.dynamic_slice_in_dim(mid_sums, place * r4, r4, axis=2)
    out_sums = jnp.concatenate([results[layer][6].reshape(1, 2, wide) for layer in range(2)])
    r6 = gains_out.shape[1]
    outs = lax.dynamic_slice_in_dim(out_sums, place * r6, r6, axis=2)
    return (
        output,
        input_grad,
        jnp.stack(grads[0]),
        jnp.stack(grads[1]),
        jnp.stack(grads[2]),
        jnp.stack(grads[3]),
        mid[:, 1].reshape(2, 2, r4),
        mid[:, 0].reshape(2, 2, r4),
        outs[:, 1],
        outs[:, 0],
    )


def solution(mesh):
    clip_size, sp_size = mesh.shape["clip"], mesh.shape["sp"]
    inner = 2 if sp_size % 2 == 0 else 1
    split = Mesh(mesh.devices.reshape(clip_size, sp_size // inner, inner), ALL)
    return jax.shard_map(
        on_device,
        mesh=split,
        in_specs=(
            P("clip", None, SP, None, None),
            P(),
            P("clip", None, SP, None, None),
            P(None, ALL, None),
            P(None, ALL, None),
            P(None, ALL, None),
            P(None, None, ALL),
            P(None, None, ALL),
            P(None, None, ALL),
            P(None, ALL),
            P(None, ALL),
        ),
        out_specs=(
            P("clip", None, SP, None, None),
            P("clip", None, SP, None, None),
            P(None, ALL, None),
            P(None, ALL, None),
            P(None, ALL, None),
            P(None, None, ALL),
            P(None, None, ALL),
            P(None, None, ALL),
            P(None, ALL),
            P(None, ALL),
        ),
        check_vma=False,
    )
```

time: 2350 us -> 505 us (0.21)
  blocking collectives: 1240 us -> 90.2 us
  waiting for transfers between devices: 630 us -> 50.4 us
  other arithmetic: 238 us -> 17.9 us
  Pallas kernels: 0 us -> 188 us
  matrix products: 123 us -> 0 us
  starting transfers between devices: 12.2 us -> 72.7 us
    psum x18 -> x0, blocking collectives: 727 us -> none  [the longest x6 248 us: norm_back(): lax.psum((channel_sum(upstream), channel_sum(upstream * normed)), ('clip'...]
    all_gather x12 -> x0, blocking collectives: 479 us -> none  [the longest x2 87.3 us: fetch_forward(): lax.all_gather(params[2][layer], ('clip', 'sp'), axis=0, tiled=True)]
    reduce_scatter x4 -> x0, waiting for transfers between devices: 364 us -> none  [the longest x2 265 us: backward_block(): lax.psum_scatter(grad_third, ('clip', 'sp'), scatter_dimension=0, tiled=T...]
    unnamed x8 -> x0, waiting for transfers between devices: 263 us -> none
    pallas_call x0 -> x13, Pallas kernels: none -> 188 us  [the longest x2 35.5 us: on_device(): call(functools.partial(depth_back_kernel, dims3, layer), (clips,), [smem(...]
    reduce_sum x14 -> x4, other arithmetic: 126 us -> 1.67 us  [the longest x1 0.71 us: on_device(): own = jnp.sum(local).astype(F32) * (rows * columns)]
    dot_general x18 -> x0, matrix products: 123 us -> none  [the longest x6 53.4 us: back_product(): lax.dot_general(grad_field, weight, (((4,), (1,)), ((), ())), preferred_e...]
    all_to_all x0 -> x5, blocking collectives: none -> 90.2 us  [the longest x4 49.6 us: share(): lax.all_to_all(jnp.broadcast_to(row[None], (peers,) + row.shape), ALL, 0, 0)]
  transfers between devices with their start and end apart: 14 -> 23, of which waited for: 6 -> 10; matrix products, arithmetic and copies ran while one was open for 7% -> 11% of each run, Pallas kernels for 0% -> 4%
where the time goes in v1:
time: 505 us; the launch traced here: 495 us
  Pallas kernels  188 us (37%)
  blocking collectives  90.2 us (18%)
  starting transfers between devices  72.7 us (14%)
  local copies, waits for them, and re-layouts  72.5 us (14%)
  waiting for transfers between devices  50.4 us (10%)
  other arithmetic  17.9 us (4%)
    all_to_all x4, blocking collectives, share(): lax.all_to_all(jnp.broadcast_to(row[None], (peers,) + row.shape), ALL, 0, 0)  49.6 us
    unnamed x82, local copies, waits for them, and re-layouts  48.8 us
    all_to_all x8, starting transfers between devices, share(): lax.all_to_all(jnp.broadcast_to(row[None], (peers,) + row.shape), ALL, 0, 0)  47.1 us
    all_to_all x8, waiting for transfers between devices, share(): lax.all_to_all(jnp.broadcast_to(row[None], (peers,) + row.shape), ALL, 0, 0)  43.3 us
    all_to_all x1, blocking collectives, on_device(): lax.all_to_all(jnp.broadcast_to(packed[None], (chips,) + packed.shape), C...  40.6 us
    pallas_call x2, Pallas kernels, on_device(): call(functools.partial(depth_back_kernel, dims3, layer), (clips,), [smem(...  35.5 us
    pallas_call x2, Pallas kernels, on_device(): call(functools.partial(mix_kernel, dims3, layer), (clips,), [smem(), smem...  25.1 us
    pallas_call x1, Pallas kernels, on_device(): call(functools.partial(cross_kernel, dims4), grid2, [smem(), smem(), line...  25 us
  transfers between devices with their start and end apart: 23, of which 10 were waited for; matrix products, arithmetic and copies ran while one was open for 11% of the time, Pallas kernels for 4%

profile of v1, /device:TPU:0, one launch (start us, length us, event | category | flops | bytes accessed | tf_op | source)
XLA Modules:
  0.0 495.4 jit_solution(13971723330096500348)
XLA Ops:
  5.9 40.6 %all_to_all.70 = bf16[16,160,256]{2,1,0:T(8,128)(2,1)S(1)} all-to-all(bf16[16,160,256]{2,1,0:T(8,128)(2,1)S(1)} %broadcast_in_dim.57), channel_id=1, replica_groups=mesh['clip'=8,'outer'=2,'inner'=2] {'clip','outer'}, dimensions={0} | all-to-all | bytes 2621440 | tf_op jit(solution)/shard_map/all_to_all | solution.py:839
  49.6 8.3 %copy.108.x_ref = bf16[4,4,7,28,1024]{4,3,2,1,0:T(8,128)(2,1)} copy(bf16[4,4,7,28,1024]{4,1,3,2,0:T(4,128)(2,1)} %param.11) | data formatting | bytes 12845056 | tf_op args[0]
  61.8 9.4 %shard_map.186 = (f32[4,4,7,32,256]{4,3,2,1,0:T(8,128)}, f32[4,4,32,256]{3,2,1,0:T(8,128)}, f32[4,4,32,256]{3,2,1,0:T(8,128)}, f32[1,512]{1,0:T(1,128)}) custom-call(s32[6]{0:T(128)} %pad_add_fusion.scal, f32[4]{0:T(128)} %pad_maximum_fusion.7.nf, bf16[4,4,7,28,1024]{4,3,2,1,0:T(8,128)(2,1)} %copy.108.x_ref, bf16[1024,256]{1,0:T(8,128)(2,1)} %bitcast.140), custom_call_target="tpu_custom_call" | custom-call | tf_op jit(solution)/shard_map/pallas_call | solution.py:892
  89.8 12.6 %shard_map.187 = (bf16[4,4,9,32,256]{4,3,2,1,0:T(8,128)(2,1)}, f32[4,4,7,32,256]{4,3,2,1,0:T(8,128)}, bf16[4,4,7,32,256]{4,3,2,1,0:T(8,128)(2,1)}, bf16[4,4,7,32...) custom-call(s32[6]{0:T(128)} %pad_add_fusion.scal, ...), custom_call_target="tpu_custom_call" | custom-call | tf_op jit(solution)/shard_map/pallas_call | solution.py:904
  103.1 11.2 %all_to_all.71.got_ref = f32[32,1,512]{2,1,0:T(1,128)} all-to-all(f32[32,1,512]{2,1,0:T(1,128)S(1)} %broadcast_in_dim.123), channel_id=1, replica_groups=mesh['clip'=8,'outer'=2,'inner'=2] {'clip','outer','inner'}, dimensions={0} | all-to-all | bytes 131072 | tf_op jit(solution)/shard_map/all_to_all | solution.py:772
  114.2 8.2 %shard_map.188 = (bf16[4,4,7,32,256]{4,3,2,1,0:T(8,128)(2,1)}, bf16[4,4,7,32,256]{4,3,2,1,0:T(8,128)(2,1)}, bf16[4,4,7,32,256]{4,3,2,1,0:T(8,128)(2,1)}, bf16[4,...) custom-call(s32[6]{0:T(128)} %pad_add_fusion.scal, ...), custom_call_target="tpu_custom_call" | custom-call | tf_op jit(solution)/shard_map/pallas_call | solution.py:917
  135.8 20.8 %shard_map.189 = (bf16[4,4,7,32,1024]{4,3,2,1,0:T(8,128)(2,1)}, bf16[4,4,7,28,1024]{4,3,2,1,0:T(8,128)(2,1)}, f32[4,4,7,32,256]{4,3,2,1,0:T(8,128)}, f32[4,4,32,...) custom-call(s32[6]{0:T(128)} %pad_add_fusion.scal, f32[4]{0:T(128)} %pad_maximum_fusion.7.nf, ...), custom_call_target="tpu_custom_call" | custom-call | tf_op jit(solution)/shard_map/pallas_call | solution.py:933
  160.9 14.2 %all_to_all.72.got_ref = f32[32,1,512]{2,1,0:T(1,128)} all-to-all(f32[32,1,512]{2,1,0:T(1,128)S(1)} %broadcast_in_dim.128), channel_id=1, replica_groups=mesh['clip'=8,'outer'=2,'inner'=2] {'clip','outer','inner'}, dimensions={0} | all-to-all | bytes 131072 | tf_op jit(solution)/shard_map/all_to_all | solution.py:772
  176.1 12.6 %shard_map.190 = (bf16[4,4,9,32,256]{4,3,2,1,0:T(8,128)(2,1)}, f32[4,4,7,32,256]{4,3,2,1,0:T(8,128)}, bf16[4,4,7,32,256]{4,3,2,1,0:T(8,128)(2,1)}, bf16[4,4,7,32...) custom-call(s32[6]{0:T(128)} %pad_add_fusion.scal, ...), custom_call_target="tpu_custom_call" | custom-call | tf_op jit(solution)/shard_map/pallas_call | solution.py:904
  189.4 11.2 %all_to_all.73.got_ref = f32[32,1,512]{2,1,0:T(1,128)} all-to-all(f32[32,1,512]{2,1,0:T(1,128)S(1)} %broadcast_in_dim.130), channel_id=1, replica_groups=mesh['clip'=8,'outer'=2,'inner'=2] {'clip','outer','inner'}, dimensions={0} | all-to-all | bytes 131072 | tf_op jit(solution)/shard_map/all_to_all | solution.py:772
  200.5 8.2 %shard_map.191 = (bf16[4,4,7,32,256]{4,3,2,1,0:T(8,128)(2,1)}, bf16[4,4,7,32,256]{4,3,2,1,0:T(8,128)(2,1)}, bf16[4,4,7,32,256]{4,3,2,1,0:T(8,128)(2,1)}, bf16[4,...) custom-call(s32[6]{0:T(128)} %pad_add_fusion.scal, ...), custom_call_target="tpu_custom_call" | custom-call | tf_op jit(solution)/shard_map/pallas_call | solution.py:917
  212.8 8.4 %copy.109.cot_ref = bf16[4,4,7,28,1024]{4,3,2,1,0:T(8,128)(2,1)} copy(bf16[4,4,7,28,1024]{4,1,3,2,0:T(4,128)(2,1)} %param.13) | data formatting | bytes 12845056 | tf_op args[2]
  222.0 23.8 %shard_map.192 = (bf16[4,4,7,28,1024]{4,3,2,1,0:T(8,128)(2,1)}, bf16[4,4,7,28,1024]{4,3,2,1,0:T(8,128)(2,1)}, f32[4,4,7,32,256]{4,3,2,1,0:T(8,128)}, f32[264,102...) custom-call(s32[6]{0:T(128)} %pad_add_fusion.scal, f32[4]{0:T(128)} %pad_maximum_fusion.7.nf, ...), custom_call_target="tpu_custom_call" | custom-call | tf_op jit(solution)/shard_map/pallas_call | solution.py:943
  265.6 8.7 %shard_map.193 = (bf16[4,4,7,32,256]{4,3,2,1,0:T(8,128)(2,1)}, bf16[4,4,32,256]{3,2,1,0:T(8,128)(2,1)}, bf16[4,4,32,256]{3,2,1,0:T(8,128)(2,1)}, f32[1,512]{1,0:...) custom-call(s32[6]{0:T(128)} %pad_add_fusion.scal, f32[4]{0:T(128)} %pad_maximum_fusion.7.nf, ...), custom_call_target="tpu_custom_call" | custom-call | tf_op jit(solution)/shard_map/pallas_call | solution.py:958
  279.0 14.4 %all-to-all-start.8 = ((f32[32,1,512]{2,1,0:T(1,128)}), f32[32,1,512]{2,1,0:T(1,128)S(1)}, u32[]{:S(2)}, u32[]{:S(2)}) async-start(f32[32,1,512]{2,1,0:T(1,128)} %broadcast_in_dim.136), calls=%async_computation.8 | async-start | bytes 131072 | tf_op jit(solution)/shard_map/all_to_all | solution.py:772
  301.4 17.8 %shard_map.194 = (bf16[4,4,7,32,256]{4,3,2,1,0:T(8,128)(2,1)}, f32[1,512]{1,0:T(1,128)}, f32[256,256]{1,0:T(8,128)}, f32[32,256]{1,0:T(8,128)}, f32[1,512]{1,0:T(1,128)}) custom-call(s32[6]{0:T(128)} %pad_add_fusion.scal, f32[4]{0:T(128)} %pad_maximum_fusion.7.nf, bf16[4,4,7,32,256]{4,3,2,1,0:T(8,128)(2,1)} %get-tuple-element.113.go_ref, ...), custom_call_target="tpu_custom_call" | custom-call | tf_op jit(solution)/shard_map/pallas_call | solution.py:972
  319.9 13.0 %all_to_all.74.got_ref = f32[32,1,512]{2,1,0:T(1,128)} all-to-all(f32[32,1,512]{2,1,0:T(1,128)S(1)} %broadcast_in_dim.138), channel_id=1, replica_groups=mesh['clip'=8,'outer'=2,'inner'=2] {'clip','outer','inner'}, dimensions={0} | all-to-all | bytes 131072 | tf_op jit(solution)/shard_map/all_to_all | solution.py:772
  332.9 25.0 %shard_map.195 = (bf16[4,4,7,28,1024]{4,3,2,1,0:T(8,128)(2,1)}, f32[4,4,7,32,256]{4,3,2,1,0:T(8,128)}, f32[264,1024]{1,0:T(8,128)}, f32[1,2048]{1,0:T(1,128)}, b...) custom-call(s32[6]{0:T(128)} %pad_add_fusion.scal, f32[4]{0:T(128)} %pad_maximum_fusion.7.nf, ...), custom_call_target="tpu_custom_call" | custom-call | tf_op jit(solution)/shard_map/pallas_call | solution.py:992
  375.5 8.7 %shard_map.196 = (bf16[4,4,7,32,256]{4,3,2,1,0:T(8,128)(2,1)}, bf16[4,4,32,256]{3,2,1,0:T(8,128)(2,1)}, bf16[4,4,32,256]{3,2,1,0:T(8,128)(2,1)}, f32[1,512]{1,0:...) custom-call(s32[6]{0:T(128)} %pad_add_fusion.scal, f32[4]{0:T(128)} %pad_maximum_fusion.7.nf, ...), custom_call_target="tpu_custom_call" | custom-call | tf_op jit(solution)/shard_map/pallas_call | solution.py:958
  394.2 7.2 %all-to-all-done.11.got_ref = f32[32,1,512]{2,1,0:T(1,128)S(1)} async-done(((f32[32,1,512]{2,1,0:T(1,128)}), f32[32,1,512]{2,1,0:T(1,128)S(1)}, u32[]{:S(2)}, u32[]{:S(2)}) %all-to-all-start.11) | async-done | bytes 65568 | tf_op jit(solution)/shard_map/all_to_all | solution.py:772
  402.2 17.7 %shard_map.197 = (bf16[4,4,7,32,256]{4,3,2,1,0:T(8,128)(2,1)}, f32[1,512]{1,0:T(1,128)}, f32[256,256]{1,0:T(8,128)}, f32[32,256]{1,0:T(8,128)}, f32[1,512]{1,0:T(1,128)}) custom-call(s32[6]{0:T(128)} %pad_add_fusion.scal, f32[4]{0:T(128)} %pad_maximum_fusion.7.nf, bf16[4,4,7,32,256]{4,3,2,1,0:T(8,128)(2,1)} %get-tuple-element.136.go_ref, ...), custom_call_target="tpu_custom_call" | custom-call | tf_op jit(solution)/shard_map/pallas_call | solution.py:972
  435.0 15.1 %shard_map.198 = (bf16[4,4,7,28,1024]{4,3,2,1,0:T(8,128)(2,1)}, bf16[1024,256]{1,0:T(8,128)(2,1)}, f32[1,512]{1,0:T(1,128)}) custom-call(s32[6]{0:T(128)} %pad_add_fusion.scal, f32[4]{0:T(128)} %pad_maximum_fusion.7.nf, bf16[4,4,7,32,256]{4,3,2,1,0:T(8,128)(2,1)} %get-tuple-element.147.go_ref, bf16[4,4,7,32,256]{4,3,2,1,0:T(8,128)(2,1)} %get-tuple-element.145.z1_ref.z_ref, ...), custom_call_target="tpu_custom_call" | custom-call | tf_op jit(solution)/shard_map/pallas_call | solution.py:1007
  463.4 11.8 %copy.117 = bf16[4,4,7,28,1024]{4,1,3,2,0:T(4,128)(2,1)} copy(bf16[4,4,7,28,1024]{4,3,2,1,0:T(8,128)(2,1)} %get-tuple-element.196) | data formatting | bytes 12845056
  475.9 11.8 %copy.118 = bf16[4,4,7,28,1024]{4,1,3,2,0:T(4,128)(2,1)} copy(bf16[4,4,7,28,1024]{4,3,2,1,0:T(8,128)(2,1)} %get-tuple-element.197) | data formatting | bytes 12845056
  (206 shorter events, 151.6 us)
Async XLA Ops:
  0.6 45.9 %copy-start.32 = (s32[32]{0:T(128)S(1)}, s32[32]{0:T(128)}, u32[]{:S(2)}) copy-start(s32[32]{0:T(128)} %param.12) | copy-start | bytes 388
  46.5 13.3 %collective-permute-start = (bf16[16,160,256]{2,1,0:T(8,128)(2,1)S(1)}, bf16[16,160,256]{2,1,0:T(8,128)(2,1)S(1)}, u32[]{:S(2)}, u32[]{:S(2)}) collective-permute-start(bf16[16,160,256]{2,1,0:T(8,128)(2,1)S(1)} %all_to_all.70), channel_id=1, source_target_pairs={{0,1},{1,0},{2,3},{3,2},{4,5},{5,4},{6,7},{7,6},{8,9},{9,8},{10,11... | collective-permute-start | bytes 3932168 | tf_op jit(solution)/shard_map/ppermute | solution.py:785
  71.2 17.7 %collective-permute-start.1 = (f32[4,4,32,256]{3,2,1,0:T(8,128)}, f32[4,4,32,256]{3,2,1,0:T(8,128)S(1)}, u32[]{:S(2)}, u32[]{:S(2)}) collective-permute-start(f32[4,4,32,256]{3,2,1,0:T(8,128)} %get-tuple-element.89), channel_id=1, source_target_pairs={{0,1},{1,2},{2,3},{4,5},{5,6},{6,7},{8,9},{9,10},{10,11},{12,13},{... | collective-permute-start | bytes 1572872 | tf_op jit(solution)/shard_map/ppermute | solution.py:778
  73.7 15.3 %collective-permute-start.2 = (f32[4,4,32,256]{3,2,1,0:T(8,128)}, f32[4,4,32,256]{3,2,1,0:T(8,128)}, u32[]{:S(2)}, u32[]{:S(2)}) collective-permute-start(f32[4,4,32,256]{3,2,1,0:T(8,128)} %get-tuple-element.90), channel_id=1, source_target_pairs={{1,0},{2,1},{3,2},{5,4},{6,5},{7,6},{9,8},{10,9},{11,10},{13,12},{... | collective-permute-start | bytes 1572872 | tf_op jit(solution)/shard_map/ppermute | solution.py:779
  77.2 11.7 %all-to-all-start.1 = ((f32[32,1,512]{2,1,0:T(1,128)}), f32[32,1,512]{2,1,0:T(1,128)S(1)}, u32[]{:S(2)}, u32[]{:S(2)}) async-start(f32[32,1,512]{2,1,0:T(1,128)} %broadcast_in_dim.59), calls=%async_computation.1 | async-start | bytes 131072 | tf_op jit(solution)/shard_map/all_to_all | solution.py:772
  123.9 11.2 %all-to-all-start.3 = ((f32[32,1,1280]{2,1,0:T(1,128)}), f32[32,1,1280]{2,1,0:T(1,128)S(1)}, u32[]{:S(2)}, u32[]{:S(2)}) async-start(f32[32,1,1280]{2,1,0:T(1,128)} %broadcast_in_dim.125), calls=%async_computation.3 | async-start | bytes 327680 | tf_op jit(solution)/shard_map/all_to_all | solution.py:772
  156.5 18.6 %collective-permute-start.3 = (f32[4,4,32,256]{3,2,1,0:T(8,128)}, f32[4,4,32,256]{3,2,1,0:T(8,128)S(1)}, u32[]{:S(2)}, u32[]{:S(2)}) collective-permute-start(f32[4,4,32,256]{3,2,1,0:T(8,128)} %get-tuple-element.98), channel_id=1, source_target_pairs={{0,1},{1,2},{2,3},{4,5},{5,6},{6,7},{8,9},{9,10},{10,11},{12,13},{... | collective-permute-start | bytes 1572872 | tf_op jit(solution)/shard_map/ppermute | solution.py:778
  158.9 16.2 %collective-permute-start.4 = (f32[4,4,32,256]{3,2,1,0:T(8,128)}, f32[4,4,32,256]{3,2,1,0:T(8,128)S(1)}, u32[]{:S(2)}, u32[]{:S(2)}) collective-permute-start(f32[4,4,32,256]{3,2,1,0:T(8,128)} %get-tuple-element.99), channel_id=1, source_target_pairs={{1,0},{2,1},{3,2},{5,4},{6,5},{7,6},{9,8},{10,9},{11,10},{13,12},{... | collective-permute-start | bytes 1572872 | tf_op jit(solution)/shard_map/ppermute | solution.py:779
  210.2 11.2 %all-to-all-start.6 = ((f32[32,1,1280]{2,1,0:T(1,128)}), f32[32,1,1280]{2,1,0:T(1,128)S(1)}, u32[]{:S(2)}, u32[]{:S(2)}) async-start(f32[32,1,1280]{2,1,0:T(1,128)} %broadcast_in_dim.132), calls=%async_computation.6 | async-start | bytes 327680 | tf_op jit(solution)/shard_map/all_to_all | solution.py:772
  249.4 15.3 %all-to-all-start.7 = ((bf16[32,2,1024]{2,1,0:T(2,128)(2,1)}), bf16[32,2,1024]{2,1,0:T(2,128)(2,1)S(1)}, u32[]{:S(2)}, u32[]{:S(2)}) async-start(bf16[32,2,1024]{2,1,0:T(2,128)(2,1)} %reshape.237), calls=%async_computation.7 | async-start | bytes 262144 | tf_op jit(solution)/shard_map/all_to_all | solution.py:772
  256.5 36.9 %collective-permute-start.7 = (bf16[4,4,32,256]{3,2,1,0:T(8,128)(2,1)S(1)}, bf16[4,4,32,256]{3,2,1,0:T(8,128)(2,1)S(1)}, u32[]{:S(2)}, u32[]{:S(2)}) collective-permute-start(bf16[4,4,32,256]{3,2,1,0:T(8,128)(2,1)S(1)} %copy-done.31), channel_id=1, source_target_pairs={{0,1},{1,2},{2,3},{4,5},{5,6},{6,7},{8,9},{9,10},{10,11},{12,13},{... | collective-permute-start | bytes 786440 | tf_op jit(solution)/shard_map/ppermute | solution.py:778
  258.7 34.7 %collective-permute-start.8 = (bf16[4,4,32,256]{3,2,1,0:T(8,128)(2,1)S(1)}, bf16[4,4,32,256]{3,2,1,0:T(8,128)(2,1)S(1)}, u32[]{:S(2)}, u32[]{:S(2)}) collective-permute-start(bf16[4,4,32,256]{3,2,1,0:T(8,128)(2,1)S(1)} %copy-done.30), channel_id=1, source_target_pairs={{1,0},{2,1},{3,2},{5,4},{6,5},{7,6},{9,8},{10,9},{11,10},{13,12},{... | collective-permute-start | bytes 786440 | tf_op jit(solution)/shard_map/ppermute | solution.py:779
  274.2 26.3 %collective-permute-start.5 = (bf16[4,4,32,256]{3,2,1,0:T(8,128)(2,1)}, bf16[4,4,32,256]{3,2,1,0:T(8,128)(2,1)S(1)}, u32[]{:S(2)}, u32[]{:S(2)}) collective-permute-start(bf16[4,4,32,256]{3,2,1,0:T(8,128)(2,1)} %get-tuple-element.114), channel_id=1, source_target_pairs={{0,1},{1,2},{2,3},{4,5},{5,6},{6,7},{8,9},{9,10},{10,11},{12,13},{... | collective-permute-start | bytes 786440 | tf_op jit(solution)/shard_map/ppermute | solution.py:778
  276.4 24.2 %collective-permute-start.6 = (bf16[4,4,32,256]{3,2,1,0:T(8,128)(2,1)}, bf16[4,4,32,256]{3,2,1,0:T(8,128)(2,1)S(1)}, u32[]{:S(2)}, u32[]{:S(2)}) collective-permute-start(bf16[4,4,32,256]{3,2,1,0:T(8,128)(2,1)} %get-tuple-element.115), channel_id=1, source_target_pairs={{1,0},{2,1},{3,2},{5,4},{6,5},{7,6},{9,8},{10,9},{11,10},{13,12},{... | collective-permute-start | bytes 786440 | tf_op jit(solution)/shard_map/ppermute | solution.py:779
  279.0 21.5 %all-to-all-start.8 = ((f32[32,1,512]{2,1,0:T(1,128)}), f32[32,1,512]{2,1,0:T(1,128)S(1)}, u32[]{:S(2)}, u32[]{:S(2)}) async-start(f32[32,1,512]{2,1,0:T(1,128)} %broadcast_in_dim.136), calls=%async_computation.8 | async-start | bytes 131072 | tf_op jit(solution)/shard_map/all_to_all | solution.py:772
  361.0 13.7 %all-to-all-start.10 = ((bf16[32,2,1024]{2,1,0:T(2,128)(2,1)}), bf16[32,2,1024]{2,1,0:T(2,128)(2,1)S(1)}, u32[]{:S(2)}, u32[]{:S(2)}) async-start(bf16[32,2,1024]{2,1,0:T(2,128)(2,1)} %reshape.239), calls=%async_computation.10 | async-start | bytes 262144 | tf_op jit(solution)/shard_map/all_to_all | solution.py:772
  366.4 27.7 %collective-permute-start.11 = (bf16[4,4,32,256]{3,2,1,0:T(8,128)(2,1)S(1)}, bf16[4,4,32,256]{3,2,1,0:T(8,128)(2,1)S(1)}, u32[]{:S(2)}, u32[]{:S(2)}) collective-permute-start(bf16[4,4,32,256]{3,2,1,0:T(8,128)(2,1)S(1)} %copy-done.29), channel_id=1, source_target_pairs={{0,1},{1,2},{2,3},{4,5},{5,6},{6,7},{8,9},{9,10},{10,11},{12,13},{... | collective-permute-start | bytes 786440 | tf_op jit(solution)/shard_map/ppermute | solution.py:778
  368.6 25.6 %collective-permute-start.12 = (bf16[4,4,32,256]{3,2,1,0:T(8,128)(2,1)S(1)}, bf16[4,4,32,256]{3,2,1,0:T(8,128)(2,1)S(1)}, u32[]{:S(2)}, u32[]{:S(2)}) collective-permute-start(bf16[4,4,32,256]{3,2,1,0:T(8,128)(2,1)S(1)} %copy-done.28), channel_id=1, source_target_pairs={{1,0},{2,1},{3,2},{5,4},{6,5},{7,6},{9,8},{10,9},{11,10},{13,12},{... | collective-permute-start | bytes 786440 | tf_op jit(solution)/shard_map/ppermute | solution.py:779
  384.2 17.2 %collective-permute-start.9 = (bf16[4,4,32,256]{3,2,1,0:T(8,128)(2,1)}, bf16[4,4,32,256]{3,2,1,0:T(8,128)(2,1)S(1)}, u32[]{:S(2)}, u32[]{:S(2)}) collective-permute-start(bf16[4,4,32,256]{3,2,1,0:T(8,128)(2,1)} %get-tuple-element.137), channel_id=1, source_target_pairs={{0,1},{1,2},{2,3},{4,5},{5,6},{6,7},{8,9},{9,10},{10,11},{12,13},{... | collective-permute-start | bytes 786440 | tf_op jit(solution)/shard_map/ppermute | solution.py:778
  386.3 15.0 %collective-permute-start.10 = (bf16[4,4,32,256]{3,2,1,0:T(8,128)(2,1)}, bf16[4,4,32,256]{3,2,1,0:T(8,128)(2,1)S(1)}, u32[]{:S(2)}, u32[]{:S(2)}) collective-permute-start(bf16[4,4,32,256]{3,2,1,0:T(8,128)(2,1)} %get-tuple-element.138), channel_id=1, source_target_pairs={{1,0},{2,1},{3,2},{5,4},{6,5},{7,6},{9,8},{10,9},{11,10},{13,12},{... | collective-permute-start | bytes 786440 | tf_op jit(solution)/shard_map/ppermute | solution.py:779
  389.0 12.4 %all-to-all-start.11 = ((f32[32,1,512]{2,1,0:T(1,128)}), f32[32,1,512]{2,1,0:T(1,128)S(1)}, u32[]{:S(2)}, u32[]{:S(2)}) async-start(f32[32,1,512]{2,1,0:T(1,128)} %broadcast_in_dim.142), calls=%async_computation.11 | async-start | bytes 131072 | tf_op jit(solution)/shard_map/all_to_all | solution.py:772
  421.3 13.1 %all-to-all-start.12 = ((f32[32,1,512]{2,1,0:T(1,128)}), f32[32,1,512]{2,1,0:T(1,128)S(1)}, u32[]{:S(2)}, u32[]{:S(2)}) async-start(f32[32,1,512]{2,1,0:T(1,128)} %broadcast_in_dim.144), calls=%async_computation.12 | async-start | bytes 131072 | tf_op jit(solution)/shard_map/all_to_all | solution.py:772
  452.8 3.4 collective-permute-start.13
  459.0 33.3 %all-to-all-start.13 = ((bf16[16,160,256]{2,1,0:T(8,128)(2,1)}), bf16[16,160,256]{2,1,0:T(8,128)(2,1)S(1)}, u32[]{:S(2)}, u32[]{:S(2)}) async-start(bf16[16,160,256]{2,1,0:T(8,128)(2,1)} %fusion), calls=%async_computation.13 | async-start | bytes 2621440 | tf_op jit(solution)/shard_map/all_to_all | solution.py:1032
  (32 other events, 306.3 us)
